TPU v7x, 32 devices: a whole 2x2x4 slice. The times are simulated.
32 devices in a mesh: seq: 16 (over z, y, x), ch: 2 (over core).
Axes of the slice: x: 2, y: 2, z: 4, core: 2. Of those that a mesh axis runs over, the one named last changes fastest.
Arguments:
- gate_input: bfloat16 [4096, 4096], P('seq', 'ch'), may hold values from -6 to 6
- key_input: bfloat16 [4096, 4096], P('seq', 'ch'), may hold values from -6 to 6
- value_input: bfloat16 [4096, 4096], P('seq', 'ch'), may hold values from -6 to 6
- decay_rate: float32 [4096, 16], P('ch'), as said below
- residues: float32 [4096, 16], P('ch'), may hold values from -1.5 to 1.5
- out_weight: bfloat16 [4096, 4096], P('ch', 'seq'), may hold values from -0.09375 to 0.09375
Outputs:
- mixed: bfloat16 [4096, 4096], P(('seq', 'ch'))
Inputs may be any that keep to these rules, and one draw needn't show every extreme that they name: `decay_rate`: every entry is positive and at most 0.05.
All inputs are finite; a program needn't handle non-finite values.
Results may differ from a plain program's by a relative error of at most 0.025.
Values may be sent and summed in bfloat16 or wider, within the bound.
A program may use at most 128 MiB of HBM per device.

v0:
```python
import math

import jax
import jax.numpy as jnp
from jax import lax
from jax.sharding import PartitionSpec as P

exact_mode = lax.Precision.HIGHEST


def cos_sin(products, period):
    angles = 2.0 * math.pi / period * (products % period).astype(jnp.float32)
    return (jnp.cos(angles), jnp.sin(angles))


def transform_conv(signal, decay_rate, residues, shards, my_index, length, chans):
    per_piece = length // shards
    tokens_all = shards * length
    full_len = 2 * tokens_all
    pole_count = residues.shape[1]
    places = (my_index * length + jnp.arange(length)).astype(jnp.float32)[:, None]

    def add_pole(pole_idx, impulse):
        rate = lax.dynamic_index_in_dim(decay_rate, pole_idx, 1, keepdims=False)
        weight_pole = lax.dynamic_index_in_dim(residues, pole_idx, 1, keepdims=False)
        amplitude = weight_pole * jnp.sqrt(rate)
        return impulse + amplitude[None, :] * jnp.exp(-rate[None, :] * places)

    impulse = lax.fori_loop(0, pole_count, add_pole, jnp.zeros((length, chans), jnp.float32))
    stacked = jnp.stack([signal, impulse])
    copies = stacked.shape[0]
    outgoing = stacked.reshape(copies, shards, per_piece, chans)
    arrived = lax.all_to_all(
        outgoing.astype(jnp.bfloat16), "seq", split_axis=1, concat_axis=1, tiled=True
    ).astype(outgoing.dtype)
    freq_block = jnp.arange(2 * shards)
    cos_b, sin_b = cos_sin(freq_block[:, None] * jnp.arange(shards)[None, :], 2 * shards)
    flat = arrived.reshape(copies, shards, per_piece * chans)
    real_b = jnp.einsum("ks,fsx->fkx", cos_b, flat, precision=exact_mode).reshape(
        copies, 2 * shards, per_piece, chans
    )
    imag_b = -jnp.einsum("ks,fsx->fkx", sin_b, flat, precision=exact_mode).reshape(
        copies, 2 * shards, per_piece, chans
    )
    local_steps = my_index * per_piece + jnp.arange(per_piece)
    cos_w, sin_w = cos_sin(freq_block[:, None] * local_steps[None, :], full_len)
    cos_w = cos_w[None, :, :, None]
    sin_w = sin_w[None, :, :, None]
    turned_re = real_b * cos_w + imag_b * sin_w
    turned_im = imag_b * cos_w - real_b * sin_w
    spectral = jnp.stack([turned_re, turned_im]).reshape(2, copies, 2, shards, per_piece, chans)
    columns = (
        lax.all_to_all(
            spectral.astype(jnp.bfloat16), "seq", split_axis=3, concat_axis=3, tiled=True
        )
        .astype(spectral.dtype)
        .reshape(2, copies, 2, length, chans)
    )
    all_steps = jnp.arange(length)
    cos_c, sin_c = cos_sin(all_steps[:, None] * all_steps[None, :], length)
    spec_re = jnp.einsum("qt,fmtc->fmqc", cos_c, columns[0], precision=exact_mode) + jnp.einsum(
        "qt,fmtc->fmqc", sin_c, columns[1], precision=exact_mode
    )
    spec_im = jnp.einsum("qt,fmtc->fmqc", cos_c, columns[1], precision=exact_mode) - jnp.einsum(
        "qt,fmtc->fmqc", sin_c, columns[0], precision=exact_mode
    )
    owned = jnp.stack([my_index, my_index + shards])
    filt_re = spec_re[1]
    filt_im = spec_im[1]
    prod_re = spec_re[0] * filt_re - spec_im[0] * filt_im
    prod_im = spec_re[0] * filt_im + spec_im[0] * filt_re
    back_re = jnp.einsum("tq,mqc->mtc", cos_c, prod_re, precision=exact_mode) - jnp.einsum(
        "tq,mqc->mtc", sin_c, prod_im, precision=exact_mode
    )
    back_im = jnp.einsum("tq,mqc->mtc", cos_c, prod_im, precision=exact_mode) + jnp.einsum(
        "tq,mqc->mtc", sin_c, prod_re, precision=exact_mode
    )
    cos_v, sin_v = cos_sin(owned[:, None] * all_steps[None, :], full_len)
    cos_v = cos_v[:, :, None]
    sin_v = sin_v[:, :, None]
    rot_re = back_re * cos_v - back_im * sin_v
    rot_im = back_re * sin_v + back_im * cos_v
    returning = jnp.stack([rot_re, rot_im]).reshape(2, 2, shards, per_piece, chans)
    returned = (
        lax.all_to_all(
            returning.astype(jnp.bfloat16), "seq", split_axis=2, concat_axis=2, tiled=True
        )
        .astype(returning.dtype)
        .reshape(2, 2 * shards, per_piece * chans)
    )
    finished = (
        jnp.einsum("ks,kx->sx", cos_b, returned[0], precision=exact_mode)
        - jnp.einsum("ks,kx->sx", sin_b, returned[1], precision=exact_mode)
    ) / full_len
    return (
        lax.all_to_all(
            finished.reshape(shards, per_piece, chans).astype(jnp.bfloat16),
            "seq",
            split_axis=0,
            concat_axis=0,
            tiled=True,
        )
        .astype(jnp.float32)
        .reshape(length, chans)
    )


def body(gate_input, key_input, value_input, decay_rate, residues, out_weight):
    shards = lax.axis_size("seq")
    my_index = lax.axis_index("seq")
    length, chans = gate_input.shape
    signal = key_input.astype(jnp.float32) * value_input.astype(jnp.float32)
    conv = transform_conv(signal, decay_rate, residues, shards, my_index, length, chans)
    gated = (gate_input.astype(jnp.float32) * conv).astype(jnp.bfloat16)
    weight_rows = lax.all_gather(out_weight, "seq", axis=1, tiled=True)
    return lax.psum_scatter(
        jnp.dot(gated, weight_rows, preferred_element_type=jnp.float32).astype(jnp.bfloat16),
        "ch",
        scatter_dimension=0,
        tiled=True,
    )


def solution(mesh):
    return jax.shard_map(
        body,
        mesh=mesh,
        in_specs=(
            P("seq", "ch"),
            P("seq", "ch"),
            P("seq", "ch"),
            P("ch", None),
            P("ch", None),
            P("ch", "seq"),
        ),
        out_specs=P(("seq", "ch"), None),
        check_vma=False,
    )
```

profile of v0, /device:TPU:0, one launch (start us, length us, event | category | flops | bytes accessed | tf_op | source)
XLA Modules:
  0.0 670.3 jit_solution(4591782390191733667)
XLA Ops:
  6.5 33.6 %while.14 = (s32[]{:T(128)}, f32[256,2048]{1,0:T(8,128)S(1)}, f32[2048,16]{0,1:T(8,128)}, f32[2048,16]{0,1:T(8,128)}, s32[]{:T(128)}, /*index=5*/s32[]{:T(128)}, s32[]{:T(128)}) while((s32[]{:T(128)}, f32[256,2048]{1,0:T(8,128)S(1)}, f32[2048,16]{0,1:T(8,128)}, f32[2048,16]{0,1:T(8,128)}, s32[]{:T(128)}, /*index=5*/s32[]{:T(128)}, ...), condition=%wide.region_1.2_spmd.clone, body=%wide.region_0.1_spmd.clone.sunk | while | flops 2101763 | bytes 4245599 | solution.py:29
  11.7 1.1 select_add_fusion.2
  40.3 1.6 multiply_convert_fusion
  41.9 1.5 pad_maximum_fusion.2
  43.4 8.4 %all-to-all-start = ((bf16[2,16,16,2048]{3,2,0,1:T(8,128)(2,1)}), bf16[2,16,16,2048]{3,2,0,1:T(8,128)(2,1)}, u32[]{:S(2)}, u32[]{:S(2)}) async-start(bf16[2,16,16,2048]{3,2,0,1:T(8,128)(2,1)} %pad_maximum_fusion.2), calls=%async_computation | async-start | bytes 4194304 | tf_op jit(solution)/shard_map/all_to_all | solution.py:33
  52.1 42.8 %all-to-all-done = bf16[2,16,16,2048]{3,2,0,1:T(8,128)(2,1)} async-done(((bf16[2,16,16,2048]{3,2,0,1:T(8,128)(2,1)}), bf16[2,16,16,2048]{3,2,0,1:T(8,128)(2,1)}, u32[]{:S(2)}, u32[]{:S(2)}) %all-to-all-start) | async-done | bytes 2097184 | tf_op jit(solution)/shard_map/all_to_all | solution.py:33
  94.9 3.8 reshape.270
  98.7 3.9 fusion.20
  102.6 3.9 convolution_negate_fusion
  106.5 8.1 %copy.71 = f32[8,8,16,2048]{3,2,1,0:T(8,128)} copy(f32[8,8,16,2048]{3,1,2,0:T(8,128)S(1)} %bitcast.109) | data formatting | bytes 16777216
  114.6 8.0 %copy.72 = f32[8,8,16,2048]{3,2,1,0:T(8,128)} copy(f32[8,8,16,2048]{3,1,2,0:T(8,128)S(1)} %bitcast.108) | data formatting | bytes 16777216
  122.6 7.0 %add_convert_fusion.1 = (bf16[1,2,2,16,16,2048]{5,4,2,1,0,3:T(8,128)(2,1)S(1)}, bf16[1,2,2,16,16,2048]{5,4,2,1,0,3:T(8,128)(2,1)}) fusion(f32[1,2,2,16,16,2048]{5,4,3,2,1,0:T(8,128)} %bitcast.113, f32[1,2,2,16,16,2048]{5,4,3,2,1,0:T(8,128)S(1)} %bitcast.112, f32[2,16,16]{2,0,1:T(2,128)S(1)} %get-tuple-element.144, f32[2,16,16]{2,0,1:T(2,128)S(1)} %get-tuple-element.143), kind=kLoop, calls=%fused_computation.13 | loop fusion | flops 16777216 | bytes 25169920 | tf_op jit(solution)/shard_map/convert.7
  129.6 6.2 pad_maximum_fusion
  135.8 10.0 %all-to-all-start.1 = ((bf16[2,2,2,16,16,2048]{5,4,2,1,0,3:T(8,128)(2,1)}), bf16[2,2,2,16,16,2048]{5,4,2,1,0,3:T(8,128)(2,1)}, u32[]{:S(2)}, u32[]{:S(2)}) async-start(bf16[2,2,2,16,16,2048]{5,4,2,1,0,3:T(8,128)(2,1)} %pad_maximum_fusion), calls=%async_computation.1 | async-start | bytes 16777216 | tf_op jit(solution)/shard_map/all_to_all | solution.py:53
  146.8 199.0 %all-to-all-done.1 = bf16[2,2,2,16,16,2048]{5,4,2,1,0,3:T(8,128)(2,1)} async-done(((bf16[2,2,2,16,16,2048]{5,4,2,1,0,3:T(8,128)(2,1)}), bf16[2,2,2,16,16,2048]{5,4,2,1,0,3:T(8,128)(2,1)}, u32[]{:S(2)}, u32[]{:S(2)}) %all-to-all-start.1) | async-done | bytes 8388640 | tf_op jit(solution)/shard_map/all_to_all | solution.py:53
  345.8 4.1 fusion.122
  350.9 5.5 fusion.34
  356.4 8.9 %fusion.32 = f32[2,2,2048,256]{3,2,1,0:T(8,128)} fusion(bf16[2,2,256,2048]{3,2,1,0:T(8,128)(2,1)S(1)} %bitcast.106), kind=kOutput, calls=%fused_computation.49 | convolution fusion | flops 6443368448 | bytes 12582912 | tf_op jit(solution)/shard_map/qt,fmtc->fmqc/dot_general | solution.py:64
  365.4 5.8 add_bitcast_fusion
  371.2 9.7 %subtract_bitcast_fusion = f32[2,2,256,2048]{2,3,1,0:T(8,128)S(1)} fusion(f32[2,2,2048,256]{3,2,1,0:T(8,128)} %fusion.32, bf16[2,2,256,2048]{3,2,1,0:T(8,128)(2,1)S(1)} %bitcast.105), kind=kOutput, calls=%fused_computation.10 | convolution fusion | flops 6445465600 | bytes 20971520 | tf_op jit(solution)/shard_map/qt,fmtc->fmqc/dot_general | solution.py:64
  380.9 1.6 multiply_subtract_fusion
  382.4 4.9 fusion.6
  387.3 5.3 fusion.4
  392.6 5.7 fusion.12
  398.3 10.5 %subtract_convert_fusion.1 = (bf16[2,2048,256]{1,2,0:T(8,128)(2,1)S(1)}, bf16[2,2048,256]{1,2,0:T(8,128)(2,1)S(1)}) fusion(f32[2,2048,256]{1,2,0:T(8,128)S(1)} %fusion.12, f32[2,256]{1,0:T(2,128)S(1)} %get-tuple-element.146, f32[2,256]{1,0:T(2,128)S(1)} %get-tuple-element.145, f32[2,2048,256]{1,2,0:T(8,128)S(1)} %fusion.4, ...), kind=kOutput, calls=%fused_computation.25 | convolution fusion | flops 3231580160 | bytes 16781312 | tf_op jit(solution)/shard_map/tq,mqc->mtc/dot_general | solution.py:75
  409.8 198.9 %all_to_all.20 = bf16[2,2,16,16,2048]{4,3,1,0,2:T(8,128)(2,1)S(1)} all-to-all(bf16[2,2,16,16,2048]{4,3,1,0,2:T(8,128)(2,1)S(1)} %copy.68), channel_id=1, replica_groups=mesh['seq'=16,'ch'=2] {'seq'}, dimensions={2} | all-to-all | bytes 8388608 | tf_op jit(solution)/shard_map/all_to_all | solution.py:85
  609.4 1.2 copy.73
  610.8 1.2 copy.74
  613.0 1.2 fusion.3
  614.8 28.9 %all_to_all.21 = bf16[16,16,2048]{2,1,0:T(8,128)(2,1)S(1)} all-to-all(bf16[16,16,2048]{2,1,0:T(8,128)(2,1)S(1)} %bitcast.123), channel_id=1, replica_groups=mesh['seq'=16,'ch'=2] {'seq'}, dimensions={0} | all-to-all | bytes 2097152 | tf_op jit(solution)/shard_map/all_to_all | solution.py:96
  643.7 11.4 %convolution_convert_fusion = bf16[256,4096]{1,0:T(8,128)(2,1)} fusion(bf16[2048,4096]{1,0:T(8,128)(2,1)} %all-gather.2.cloned.1.call-done, bf16[256,2048]{1,0:T(8,128)(2,1)S(1)} %bitcast.124, bf16[256,2048]{1,0:T(8,128)(2,1)S(1)} %copy-done.1), kind=kOutput, calls=%fused_computation.14 | convolution fusion | flops 4298113024 | bytes 20971520 | tf_op jit(solution)/shard_map/dot_general | solution.py:117
  655.2 8.0 %reduce-scatter.2.cloned.1.call-done = bf16[128,4096]{1,0:T(8,128)(2,1)} async-done(((bf16[256,4096]{1,0:T(8,128)(2,1)}), bf16[128,4096]{1,0:T(8,128)(2,1)}) %reduce-scatter.2.cloned.1.call-update) | async-done | bytes 1048592 | tf_op jit(solution)/shard_map/reduce_scatter | solution.py:116
  (77 shorter events, 37.7 us)
Async XLA Ops:
  6.5 33.7 %copy-start = (bf16[256,2048]{1,0:T(8,128)(2,1)S(1)}, bf16[256,2048]{1,0:T(8,128)(2,1)}, u32[]{:S(2)}) copy-start(bf16[256,2048]{1,0:T(8,128)(2,1)} %param.10) | copy-start | bytes 3145732
  43.4 51.5 %all-to-all-start = ((bf16[2,16,16,2048]{3,2,0,1:T(8,128)(2,1)}), bf16[2,16,16,2048]{3,2,0,1:T(8,128)(2,1)}, u32[]{:S(2)}, u32[]{:S(2)}) async-start(bf16[2,16,16,2048]{3,2,0,1:T(8,128)(2,1)} %pad_maximum_fusion.2), calls=%async_computation | async-start | bytes 4194304 | tf_op jit(solution)/shard_map/all_to_all | solution.py:33
  114.6 8.0 %slice-start = ((s8[8388608]{0:T(1024)(128)(4,1)}), s8[4194304]{0:T(1024)(128)(4,1)S(1)}, s32[]{:S(2)}) async-start(s8[8388608]{0:T(1024)(128)(4,1)} %bitcast.110), calls=%async_computation.7 | async-start | bytes 8388608
  114.6 8.0 %slice-start.1 = ((s8[8388608]{0:T(1024)(128)(4,1)}), s8[4194304]{0:T(1024)(128)(4,1)S(1)}, s32[]{:S(2)}) async-start(s8[8388608]{0:T(1024)(128)(4,1)} %bitcast.110), calls=%async_computation.8 | async-start | bytes 8388608
  135.8 210.1 %all-to-all-start.1 = ((bf16[2,2,2,16,16,2048]{5,4,2,1,0,3:T(8,128)(2,1)}), bf16[2,2,2,16,16,2048]{5,4,2,1,0,3:T(8,128)(2,1)}, u32[]{:S(2)}, u32[]{:S(2)}) async-start(bf16[2,2,2,16,16,2048]{5,4,2,1,0,3:T(8,128)(2,1)} %pad_maximum_fusion), calls=%async_computation.1 | async-start | bytes 16777216 | tf_op jit(solution)/shard_map/all_to_all | solution.py:53
  145.8 497.9 %all-gather.2.cloned.1.call-start = ((), (), s32[]{:S(2)}) async-start(), calls=%async_computation.5 | async-start | bytes 17825792 | tf_op jit(solution)/shard_map/all_gather | solution.py:115
  146.5 516.7 %reduce-scatter.2.cloned.1.call-start = ((), (), s32[]{:S(2)}) async-start(), calls=%async_computation.6 | async-start | bytes 3145728 | tf_op jit(solution)/shard_map/reduce_scatter | solution.py:116
  613.0 30.7 %copy-start.1 = (bf16[256,2048]{1,0:T(8,128)(2,1)S(1)}, bf16[256,2048]{1,0:T(8,128)(2,1)}, u32[]{:S(2)}) copy-start(bf16[256,2048]{1,0:T(8,128)(2,1)} %param.8) | copy-start | bytes 3145732
Sparse Core Ops, SparseCore 0:
  149.4 395.0 all-gather.1
  655.3 7.8 reduce-scatter.1
where the time goes:
time: 674 us; the launch traced here: 670 us
  waiting for transfers between devices  251 us (37%)
  blocking collectives  228 us (34%)
  matrix products  77.7 us (12%)
  other arithmetic  51.9 us (8%)
  local copies, waits for them, and re-layouts  29.3 us (4%)
  starting transfers between devices  18.5 us (3%)
  between operations  14 us (2%)
    all_to_all x1, waiting for transfers between devices, transform_conv(): lax.all_to_all(spectral.astype(jnp.bfloat16), 'seq', split_axis=3, concat...  199 us
    all_to_all x1, blocking collectives, transform_conv(): lax.all_to_all(returning.astype(jnp.bfloat16), 'seq', split_axis=2, conca...  199 us
    all_to_all x1, waiting for transfers between devices, transform_conv(): lax.all_to_all(outgoing.astype(jnp.bfloat16), 'seq', split_axis=1, concat...  42.8 us
    all_to_all x1, blocking collectives, transform_conv(): lax.all_to_all(finished.reshape(shards, per_piece, chans).astype(jnp.bflo...  28.9 us
    unnamed x15, local copies, waits for them, and re-layouts  19.9 us
    add x16, other arithmetic, add_pole(): return impulse + amplitude[None, :] * jnp.exp(-rate[None, :] * places)  18.2 us
    mul x16, other arithmetic, add_pole(): amplitude = weight_pole * jnp.sqrt(rate)  14.7 us
  transfers between devices with their start and end apart: 4, of which 3 were waited for; matrix products, arithmetic and copies ran while one was open for 10% of the time, Pallas kernels for 0%

commit v1 on v0

v1 whole, which is shorter than its diff:
```python
import functools

import jax
import jax.numpy as jnp
from jax import lax
from jax.experimental import pallas as pl
from jax.experimental.pallas import tpu as pltpu
from jax.sharding import PartitionSpec as P

SEGS = 8
LANES = 128


def shuffle_matrix(rows, back):
    steps = rows // SEGS
    row = lax.broadcasted_iota(jnp.int32, (rows, rows), 1 if back else 0)
    col = lax.broadcasted_iota(jnp.int32, (rows, rows), 0 if back else 1)
    return ((row % SEGS) * steps + row // SEGS == col).astype(jnp.float32).astype(jnp.bfloat16)


def state_kernel(k_ref, v_ref, rate_ref, amp_ref, y_ref, prefix_ref, total_ref, signal):
    rows, chans = k_ref.shape
    poles = rate_ref.shape[0]
    steps = rows // SEGS
    turn = shuffle_matrix(rows, False)
    signal[...] = jnp.dot(turn, k_ref[...], preferred_element_type=jnp.float32) * jnp.dot(
        turn, v_ref[...], preferred_element_type=jnp.float32
    )
    seg = lax.broadcasted_iota(jnp.int32, (SEGS, LANES), 0)

    @pl.loop(0, chans // LANES)
    def _(lane):
        here = pl.ds(pl.multiple_of(lane * LANES, LANES), LANES)
        rates = [jnp.broadcast_to(rate_ref[r : r + 1, here], (SEGS, LANES)) for r in range(poles)]
        amps = [jnp.broadcast_to(amp_ref[r : r + 1, here], (SEGS, LANES)) for r in range(poles)]
        decays = [jnp.exp(-rate) for rate in rates]

        def step(j, states):
            at = pl.ds(pl.multiple_of(j * SEGS, SEGS), SEGS)
            new = signal[at, here]
            states = [state * decay + new for state, decay in zip(states, decays)]
            terms = [state * amp for state, amp in zip(states, amps)]
            while len(terms) > 1:
                terms = [a + b for a, b in zip(terms[::2], terms[1::2])]
            y_ref[at, here] = terms[0]
            return states

        states = lax.fori_loop(
            0, steps, step, [jnp.zeros((SEGS, LANES), jnp.float32)] * poles, unroll=4
        )
        for r in range(poles):
            run = states[r]
            for hop in (1, 2, 4):
                back = jnp.where(seg >= hop, pltpu.roll(run, hop, 0), 0.0)
                run = run + back * jnp.exp(rates[r] * float(-steps * hop))
            total_ref[r : r + 1, here] = run[SEGS - 1 : SEGS, :]
            prefix_ref[r, :, here] = jnp.where(seg >= 1, pltpu.roll(run, 1, 0), 0.0)


def gate_kernel(y_ref, prefix_ref, carry_ref, gate_ref, rate_ref, amp_ref, out_ref, shuffled):
    rows, chans = gate_ref.shape
    poles = rate_ref.shape[0]
    steps = rows // SEGS
    shuffled[...] = jnp.dot(
        shuffle_matrix(rows, False), gate_ref[...], preferred_element_type=jnp.float32
    )
    seg = lax.broadcasted_iota(jnp.int32, (SEGS, LANES), 0).astype(jnp.float32) * float(steps)

    @pl.loop(0, chans // LANES)
    def _(lane):
        here = pl.ds(pl.multiple_of(lane * LANES, LANES), LANES)
        decays, states = [], []
        for r in range(poles):
            rate = jnp.broadcast_to(rate_ref[r : r + 1, here], (SEGS, LANES))
            amp = amp_ref[r : r + 1, here]
            decays.append(jnp.exp(-rate))
            states.append(
                amp * (prefix_ref[r, :, here] + jnp.exp(-rate * seg) * carry_ref[r : r + 1, here])
            )

        def step(j, states):
            at = pl.ds(pl.multiple_of(j * SEGS, SEGS), SEGS)
            states = [state * decay for state, decay in zip(states, decays)]
            terms = list(states)
            while len(terms) > 1:
                terms = [a + b for a, b in zip(terms[::2], terms[1::2])]
            shuffled[at, here] = shuffled[at, here] * (y_ref[at, here] + terms[0])
            return states

        lax.fori_loop(0, steps, step, states, unroll=4)

    out_ref[...] = jnp.dot(
        shuffle_matrix(rows, True),
        shuffled[...].astype(jnp.bfloat16),
        preferred_element_type=jnp.float32,
    ).astype(jnp.bfloat16)


def conv_and_gate(gate_input, key_input, value_input, rates, amps):
    shards = lax.axis_size("seq")
    me = lax.axis_index("seq")
    rows, chans = gate_input.shape
    poles = rates.shape[0]
    width = min(512, chans)
    block = pl.BlockSpec((rows, width), lambda i: (0, i))
    small = pl.BlockSpec((poles, width), lambda i: (0, i))
    cube = pl.BlockSpec((poles, SEGS, width), lambda i: (0, 0, i))
    params = pltpu.CompilerParams(vmem_limit_bytes=32 * 1024 * 1024)
    y_local, prefix, total = pl.pallas_call(
        state_kernel,
        grid=(chans // width,),
        in_specs=[block, block, small, small],
        out_specs=[block, cube, small],
        out_shape=[
            jax.ShapeDtypeStruct((rows, chans), jnp.float32),
            jax.ShapeDtypeStruct((poles, SEGS, chans), jnp.float32),
            jax.ShapeDtypeStruct((poles, chans), jnp.float32),
        ],
        scratch_shapes=[pltpu.VMEM((rows, width), jnp.float32)],
        compiler_params=params,
        name="states",
    )(key_input, value_input, rates, amps)
    totals = lax.all_gather(total, "seq", axis=0)
    ago = me - 1 - jnp.arange(shards)
    far = (rows * jnp.maximum(ago, 0)).astype(jnp.float32)[:, None, None]
    carry = jnp.sum(
        jnp.where((ago >= 0)[:, None, None], jnp.exp(-rates[None] * far) * totals, 0.0), axis=0
    )
    return pl.pallas_call(
        gate_kernel,
        grid=(chans // width,),
        in_specs=[block, cube, small, block, small, small],
        out_specs=block,
        out_shape=jax.ShapeDtypeStruct((rows, chans), jnp.bfloat16),
        scratch_shapes=[pltpu.VMEM((rows, width), jnp.float32)],
        compiler_params=params,
        name="gate",
    )(y_local, prefix, carry, gate_input, rates, amps)


def groups_of(shards, free):
    fixed = sorted({i & ~free for i in range(shards)})
    return [[i for i in range(shards) if i & ~free == base] for base in fixed]


def body(gate_input, key_input, value_input, decay_rate, residues, out_weight):
    shards = lax.axis_size("seq")
    rates = decay_rate.T
    amps = residues.T * jnp.sqrt(rates)
    rows = gate_input.shape[0]
    cols = out_weight.shape[1]
    if shards != 16:
        weight = lax.all_gather(out_weight, "seq", axis=1, tiled=True)
        gated = conv_and_gate(gate_input, key_input, value_input, rates, amps)
        return lax.psum_scatter(
            jnp.dot(gated, weight, preferred_element_type=jnp.float32).astype(jnp.bfloat16),
            "ch",
            scatter_dimension=0,
            tiled=True,
        )
    by_row, by_col = groups_of(shards, 5), groups_of(shards, 10)
    weight = lax.all_gather(out_weight, "seq", axis=1, tiled=True, axis_index_groups=by_col)
    gated = conv_and_gate(gate_input, key_input, value_input, rates, amps)
    gated = lax.all_gather(gated, "seq", axis=0, tiled=True, axis_index_groups=by_row)
    part = jnp.dot(gated, weight, preferred_element_type=jnp.float32).astype(jnp.bfloat16)
    part = part.reshape(4, rows, 4 * cols)
    part = lax.psum_scatter(part, "ch", scatter_dimension=1, tiled=True)
    part = lax.all_to_all(
        part, "seq", split_axis=0, concat_axis=0, tiled=True, axis_index_groups=by_row
    )
    own = part.shape[1]
    part = part.reshape(2, 2, own, 2, 2, cols)
    return part.transpose(2, 3, 0, 4, 1, 5).reshape(own, shards * cols)


def solution(mesh):
    return jax.shard_map(
        body,
        mesh=mesh,
        in_specs=(
            P("seq", "ch"),
            P("seq", "ch"),
            P("seq", "ch"),
            P("ch", None),
            P("ch", None),
            P("ch", "seq"),
        ),
        out_specs=P(("seq", "ch"), None),
        check_vma=False,
    )
```

time: 674 us -> 302 us (0.45)
  blocking collectives: 228 us -> 18.5 us
  matrix products: 77.7 us -> 9.32 us
  other arithmetic: 51.9 us -> 3.19 us
  local copies, waits for them, and re-layouts: 29.3 us -> 8.34 us
  starting transfers between devices: 18.5 us -> 0.12 us
  waiting for transfers between devices: 251 us -> 234 us
  Pallas kernels: 0 us -> 15.4 us
    all_to_all x2 -> x0, waiting for transfers between devices: 242 us -> none  [the longest x1 199 us: transform_conv(): lax.all_to_all(spectral.astype(jnp.bfloat16), 'seq', split_axis=3, concat...]
    all_gather x1 -> x3, waiting for transfers between devices: 0.01 us -> 221 us  [the longest x1 79.8 us: body(): lax.all_gather(gated, 'seq', axis=0, tiled=True, axis_index_groups=by_row)]
    all_to_all x2 -> x1, blocking collectives: 228 us -> 18.5 us  [body(): lax.all_to_all(part, 'seq', split_axis=0, concat_axis=0, tiled=True, axis...]
    dot_general x13 -> x1, matrix products: 77.7 us -> 9.32 us  [body(): jnp.dot(gated, weight, preferred_element_type=jnp.float32)]
    all_to_all x2 -> x0, starting transfers between devices: 18.4 us -> none  [the longest x1 10 us: transform_conv(): lax.all_to_all(spectral.astype(jnp.bfloat16), 'seq', split_axis=3, concat...]
    add x17 -> x0, other arithmetic: 18.2 us -> none  [the longest x16 18.2 us: add_pole(): return impulse + amplitude[None, :] * jnp.exp(-rate[None, :] * places)]
    another operation x7 -> x0, other arithmetic: 16.9 us -> none
    unnamed x15 -> x14, local copies, waits for them, and re-layouts: 19.9 us -> 4.33 us
  transfers between devices with their start and end apart: 4 -> 4, of which waited for: 3 -> 4; matrix products, arithmetic and copies ran while one was open for 10% -> 1% of each run, Pallas kernels for 0% -> 2%
where the time goes in v1:
time: 302 us
  waiting for transfers between devices  234 us (77%)
  blocking collectives  18.5 us (6%)
  Pallas kernels  15.4 us (5%)
  between operations  13.2 us (4%)
  matrix products  9.32 us (3%)
  local copies, waits for them, and re-layouts  8.34 us (3%)
  other arithmetic  3.19 us (1%)
    all_gather x1, waiting for transfers between devices, body(): lax.all_gather(gated, 'seq', axis=0, tiled=True, axis_index_groups=by_row)  79.8 us
    all_gather x1, waiting for transfers between devices, body(): lax.all_gather(out_weight, 'seq', axis=1, tiled=True, axis_index_groups=b...  78.7 us
    all_gather x1, waiting for transfers between devices, conv_and_gate(): totals = lax.all_gather(total, 'seq', axis=0)  62.7 us
    all_to_all x1, blocking collectives, body(): lax.all_to_all(part, 'seq', split_axis=0, concat_axis=0, tiled=True, axis...  18.5 us
    reduce_scatter x1, waiting for transfers between devices, body(): part = lax.psum_scatter(part, 'ch', scatter_dimension=1, tiled=True)  11.5 us
    dot_general x1, matrix products, body(): jnp.dot(gated, weight, preferred_element_type=jnp.float32)  9.32 us
    pallas_call x1, Pallas kernels, conv_and_gate(): pl.pallas_call(state_kernel, grid=(chans // width,), in_specs=[block, blo...  8.78 us
    pallas_call x1, Pallas kernels, conv_and_gate(): pl.pallas_call(gate_kernel, grid=(chans // width,), in_specs=[block, cube...  6.66 us
  transfers between devices with their start and end apart: 4, of which 4 were waited for; matrix products, arithmetic and copies ran while one was open for 1% of the time, Pallas kernels for 2%

profile of v1, /device:TPU:0, one launch (start us, length us, event | category | flops | bytes accessed | tf_op | source)
XLA Modules:
  0.0 301.7 jit_solution(17877906471997854164)
XLA Ops:
  6.5 0.0 all-gather.9.cloned.1.call-start
  6.5 1.0 bitcast_negate_fusion
  7.5 0.0 copy-start
  7.6 0.9 copy-done
  8.5 0.0 copy-start.2
  8.5 1.2 copy-done.2
  9.7 0.0 copy-start.3
  9.7 1.2 copy-done.3
  10.9 8.8 %states.1 = (f32[256,2048]{1,0:T(8,128)S(1)}, f32[16,8,2048]{2,1,0:T(8,128)S(1)}, f32[16,2048]{1,0:T(8,128)}) custom-call(bf16[256,2048]{1,0:T(8,128)(2,1)S(1)} %copy-done.2, bf16[256,2048]{1,0:T(8,128)(2,1)S(1)} %copy-done.3, f32[16,2048]{1,0:T(8,128)S(1)} %bitcast.12, f32[16,2048]{1,0:T(8,128)S(1)} %get-tuple-element.12.amp_ref), custom_call_target="tpu_custom_call" | custom-call | tf_op jit(solution)/shard_map/states/pallas_call | solution.py:109
  19.7 0.0 copy-start.5
  19.7 1.0 copy-done.5
  20.7 0.0 all-gather.9.cloned.1.call-update
  20.7 0.0 all-gather.7.cloned.1.call-start
  20.7 0.7 all-gather.7.cloned.1.call-update
  21.4 0.0 all-gather.5.cloned.1.call-start
  21.5 62.7 %all-gather.9.cloned.1.call-done = f32[256,2048]{1,0:T(8,128)} async-done(((f32[16,2048]{1,0:T(8,128)}), f32[256,2048]{1,0:T(8,128)}) %all-gather.9.cloned.1.call-update) | async-done | bytes 2097168 | tf_op jit(solution)/shard_map/all_gather | solution.py:123
  84.2 2.2 select_reduce_fusion.carry_ref
  86.4 0.0 copy-done.1
  86.4 0.0 copy-done.4
  86.4 0.0 copy-done.6
  86.4 6.7 %gate.1 = bf16[256,2048]{1,0:T(8,128)(2,1)} custom-call(f32[256,2048]{1,0:T(8,128)S(1)} %get-tuple-element.8.y_ref, f32[16,8,2048]{2,1,0:T(8,128)S(1)} %copy-done.6, f32[16,2048]{1,0:T(8,128)S(1)} %select_reduce_fusion.carry_ref, bf16[256,2048]{1,0:T(8,128)(2,1)S(1)} %copy-done.4, f32[16,2048]{1,0:T(8,128)S(1)} %bitcast.13, ...), custom_call_target="tpu_custom_call" | custom-call | tf_op jit(solution)/shard_map/gate/pallas_call | solution.py:129
  93.1 0.0 all-gather.5.cloned.1.call-update
  93.1 0.0 reduce-scatter.2.cloned.1.call-start
  93.2 78.7 %all-gather.7.cloned.1.call-done = bf16[2048,1024]{1,0:T(8,128)(2,1)} async-done(((bf16[2048,256]{1,0:T(8,128)(2,1)}), bf16[2048,1024]{1,0:T(8,128)(2,1)}) %all-gather.7.cloned.1.call-update) | async-done | bytes 4194320 | tf_op jit(solution)/shard_map/all_gather | solution.py:162
  171.9 79.8 %all-gather.5.cloned.1.call-done = bf16[1024,2048]{1,0:T(8,128)(2,1)} async-done(((bf16[256,2048]{1,0:T(8,128)(2,1)}), bf16[1024,2048]{1,0:T(8,128)(2,1)}) %all-gather.5.cloned.1.call-update) | async-done | bytes 4194320 | tf_op jit(solution)/shard_map/all_gather | solution.py:164
  251.7 9.3 %convolution_convert_fusion = bf16[1024,1024]{1,0:T(8,128)(2,1)} fusion(bf16[1024,2048]{1,0:T(8,128)(2,1)} %all-gather.5.cloned.1.call-done, bf16[2048,1024]{1,0:T(8,128)(2,1)} %all-gather.7.cloned.1.call-done), kind=kOutput, calls=%fused_computation.1 | convolution fusion | flops 4296015872 | bytes 10485760 | tf_op jit(solution)/shard_map/dot_general | solution.py:165
  261.0 0.0 reduce-scatter.2.cloned.1.call-update
  261.1 11.5 %reduce-scatter.2.cloned.1.call-done = bf16[4,128,1024]{2,1,0:T(8,128)(2,1)} async-done(((bf16[4,256,1024]{2,1,0:T(8,128)(2,1)}), bf16[4,128,1024]{2,1,0:T(8,128)(2,1)}) %reduce-scatter.2.cloned.1.call-update) | async-done | bytes 1048592 | tf_op jit(solution)/shard_map/reduce_scatter | solution.py:167
  272.6 18.5 %all_to_all.5 = bf16[4,128,1024]{2,1,0:T(8,128)(2,1)S(1)} all-to-all(bf16[4,128,1024]{2,1,0:T(8,128)(2,1)} %reduce-scatter.2.cloned.1.call-done), channel_id=1, replica_groups={{0,2,8,10},{4,6,12,14},{16,18,24,26},{20,22,28,30},{1,3,9,11},{5,7,13,1..., dimensions={0} | all-to-all | bytes 2097152 | tf_op jit(solution)/shard_map/all_to_all | solution.py:168
  291.1 0.8 reshape.22
  291.9 1.6 copy.9
  293.5 1.6 reshape.23
  (5 shorter events, 0.0 us)
Async XLA Ops:
  6.5 77.7 %all-gather.9.cloned.1.call-start = ((), (), s32[]{:S(2)}) async-start(), calls=%async_computation.5 | async-start | bytes 2228224 | tf_op jit(solution)/shard_map/all_gather | solution.py:123
  7.5 0.9 copy-start
  8.5 1.2 copy-start.2
  9.7 1.2 copy-start.3
  19.7 1.0 copy-start.5
  20.7 65.8 %copy-start.1 = (f32[2048,16]{0,1:T(8,128)S(1)}, f32[2048,16]{0,1:T(8,128)}, u32[]{:S(2)}) copy-start(f32[2048,16]{0,1:T(8,128)} %param.9) | copy-start | bytes 393220
  20.7 65.8 %copy-start.4 = (bf16[256,2048]{1,0:T(8,128)(2,1)S(1)}, bf16[256,2048]{1,0:T(8,128)(2,1)}, u32[]{:S(2)}) copy-start(bf16[256,2048]{1,0:T(8,128)(2,1)} %gate_ref.1) | copy-start | bytes 3145732
  20.7 151.2 %all-gather.7.cloned.1.call-start = ((), (), s32[]{:S(2)}) async-start(), calls=%async_computation.3 | async-start | bytes 5242880 | tf_op jit(solution)/shard_map/all_gather | solution.py:162
  21.4 230.3 %all-gather.5.cloned.1.call-start = ((), (), s32[]{:S(2)}) async-start(), calls=%async_computation.2 | async-start | bytes 5242880 | tf_op jit(solution)/shard_map/all_gather | solution.py:164
  84.2 2.2 copy-start.6
  93.1 179.4 %reduce-scatter.2.cloned.1.call-start = ((), (), s32[]{:S(2)}) async-start(), calls=%async_computation.4 | async-start | bytes 3145728 | tf_op jit(solution)/shard_map/reduce_scatter | solution.py:167
Sparse Core Ops, SparseCore 0:
  20.8 63.3 all-gather.8
  86.1 85.7 all-gather.6
  173.4 78.2 all-gather.4
  261.2 11.3 reduce-scatter.1

commit v2 on v1

--- a/solution.py
+++ b/solution.py
@@ -1,5 +1,3 @@
-import functools
-
 import jax
 import jax.numpy as jnp
 from jax import lax
@@ -138,39 +136,336 @@
     )(y_local, prefix, carry, gate_input, rates, amps)
 
 
-def groups_of(shards, free):
-    fixed = sorted({i & ~free for i in range(shards)})
-    return [[i for i in range(shards) if i & ~free == base] for base in fixed]
+MESH = pl.DeviceIdType.MESH
+X, Y, ZLO, ZHI = 1, 2, 4, 8
+ROW_MASKS = (0, X, ZLO, X | ZLO)
+COL_MASKS = (0, ZHI, Y, Y | ZHI)
+PARTS = 4
+
+
+def fused_kernel(
+    k_ref, v_ref, gate_ref, rate_ref, amp_ref, w_ref, out_ref,
+    turn, turn_back, signal, y_local, gates, prefix, carry, held, got,
+    weights, blocks, acc, to_core, from_core, final,
+    w_send, w_recv, a_send, a_recv, s_send, s_recv, c_send, c_recv, o_send, o_recv,
+):
+    rows, chans = k_ref.shape
+    poles = rate_ref.shape[0]
+    cols = w_ref.shape[1]
+    steps = rows // SEGS
+    part = chans // PARTS
+    half = rows // 2
+    me, core = lax.axis_index("seq"), lax.axis_index("ch")
+
+    barrier = pltpu.get_barrier_semaphore()
+    for mask in (X, Y, ZLO, ZHI, X | ZLO):
+        pl.semaphore_signal(barrier, inc=1, device_id={"seq": me ^ mask}, device_id_type=MESH)
+    pl.semaphore_signal(barrier, inc=1, device_id={"ch": 1 - core}, device_id_type=MESH)
+    pl.semaphore_wait(barrier, 6)
+
+    def send(src, dst, sems, place, target):
+        return pltpu.make_async_remote_copy(
+            src_ref=src,
+            dst_ref=dst,
+            send_sem=sems[0].at[place],
+            recv_sem=sems[1].at[place],
+            device_id=target,
+            device_id_type=MESH,
+        )
+
+    w_sems, a_sems, s_sems = (w_send, w_recv), (a_send, a_recv), (s_send, s_recv)
+    c_sems, o_sems = (c_send, c_recv), (o_send, o_recv)
+
+    def piece(slot, q):
+        return weights.at[slot, pl.ds(q * part, part), :]
+
+    w_zhi, w_y, w_on = [], [], []
+    for q in range(PARTS):
+        mine = w_ref.at[pl.ds(q * part, part), :]
+        w_zhi.append(send(mine, piece(1, q), w_sems, q, {"seq": me ^ ZHI}))
+        w_y.append(send(mine, piece(2, q), w_sems, PARTS + q, {"seq": me ^ Y}))
+        w_on.append(send(piece(1, q), piece(3, q), w_sems, 2 * PARTS + q, {"seq": me ^ Y}))
+    for q in range(PARTS):
+        w_zhi[q].start()
+        w_y[q].start()
+
+    turn[...] = shuffle_matrix(rows, False)
+    turn_back[...] = shuffle_matrix(rows, True)
+
+    @pl.loop(0, PARTS)
+    def _(q):
+        here = pl.ds(pl.multiple_of(q * part, part), part)
+        signal[:, here] = jnp.dot(
+            turn[...], k_ref[:, here], preferred_element_type=jnp.float32
+        ) * jnp.dot(turn[...], v_ref[:, here], preferred_element_type=jnp.float32)
+
+    seg = lax.broadcasted_iota(jnp.int32, (SEGS, LANES), 0)
+    seg_start = seg.astype(jnp.float32) * float(steps)
+    zeros = [jnp.zeros((SEGS, LANES), jnp.float32)] * poles
+
+    def tree(terms):
+        while len(terms) > 1:
+            terms = [a + b for a, b in zip(terms[::2], terms[1::2])]
+        return terms[0]
+
+    def wide(ref, r, here):
+        return jnp.broadcast_to(ref[r : r + 1, here], (SEGS, LANES))
+
+    @pl.loop(0, chans // LANES)
+    def _(lane):
+        here = pl.ds(pl.multiple_of(lane * LANES, LANES), LANES)
+        decays = [jnp.exp(-wide(rate_ref, r, here)) for r in range(poles)]
+
+        def step(j, states):
+            at = pl.ds(pl.multiple_of(j * SEGS, SEGS), SEGS)
+            new = signal[at, here]
+            return [state * decay + new for state, decay in zip(states, decays)]
+
+        states = lax.fori_loop(0, steps, step, zeros, unroll=4)
+        for r in range(poles):
+            run = states[r]
+            rate = wide(rate_ref, r, here)
+            for hop in (1, 2, 4):
+                back = jnp.where(seg >= hop, pltpu.roll(run, hop, 0), 0.0)
+                run = run + back * jnp.exp(rate * float(-steps * hop))
+            held[0, r : r + 1, here] = run[SEGS - 1 : SEGS, :]
+            prefix[r, :, here] = jnp.where(seg >= 1, pltpu.roll(run, 1, 0), 0.0)
+
+    def local_part(q):
+        @pl.loop(q * (part // LANES), (q + 1) * (part // LANES))
+        def _(lane):
+            here = pl.ds(pl.multiple_of(lane * LANES, LANES), LANES)
+            decays = [jnp.exp(-wide(rate_ref, r, here)) for r in range(poles)]
+            amps = [wide(amp_ref, r, here) for r in range(poles)]
+
+            def step(j, states):
+                at = pl.ds(pl.multiple_of(j * SEGS, SEGS), SEGS)
+                new = signal[at, here]
+                states = [state * decay + new for state, decay in zip(states, decays)]
+                y_local[at, here] = tree([state * amp for state, amp in zip(states, amps)])
+                return states
+
+            lax.fori_loop(0, steps, step, zeros, unroll=4)
+
+        here = pl.ds(q * part, part)
+        gates[:, here] = jnp.dot(turn[...], gate_ref[:, here], preferred_element_type=jnp.float32)
+
+    carry[...] = jnp.zeros_like(carry)
+    for bit in range(4):
+        swap = send(held.at[bit], got.at[bit], s_sems, bit, {"seq": me ^ (1 << bit)})
+        swap.start()
+        local_part(bit)
+        swap.wait()
+        theirs = got[bit]
+        rate = rate_ref[...]
+        later = (me // (1 << bit)) % 2
+        later_f = later.astype(jnp.float32)
+        before = (me % (1 << bit)).astype(jnp.float32) * float(rows)
+        span = float(rows << bit)
+        carry[...] = carry[...] + later_f * (jnp.exp(-rate * before) * theirs)
+        if bit < 3:
+            held[bit + 1] = held[bit] * jnp.exp(-rate * (span * (1.0 - later_f))) + theirs * jnp.exp(
+                -rate * (span * later_f)
+            )
+
+    a_x, a_z, a_on = [], [], []
+    for q in range(PARTS):
+        a_x.append(send(blocks.at[0, q], blocks.at[1, q], a_sems, q, {"seq": me ^ X}))
+        a_z.append(send(blocks.at[0, q], blocks.at[2, q], a_sems, PARTS + q, {"seq": me ^ ZLO}))
+        if q % 2 == 0:
+            a_on.append(
+                send(blocks.at[1, q], blocks.at[3, q], a_sems, 2 * PARTS + q, {"seq": me ^ ZLO})
+            )
+        else:
+            a_on.append(
+                send(blocks.at[2, q], blocks.at[3, q], a_sems, 2 * PARTS + q, {"seq": me ^ X})
+            )
+
+    def pass_weight(q):
+        w_zhi[q].wait_recv()
+        w_on[q].start()
+
+    def pass_block(q):
+        (a_x if q % 2 == 0 else a_z)[q].wait_recv()
+        a_on[q].start()
+
+    for q in range(PARTS):
+
+        @pl.loop(q * (part // LANES), (q + 1) * (part // LANES))
+        def _(lane):
+            here = pl.ds(pl.multiple_of(lane * LANES, LANES), LANES)
+            decays, states = [], []
+            for r in range(poles):
+                rate = wide(rate_ref, r, here)
+                decays.append(jnp.exp(-rate))
+                states.append(
+                    amp_ref[r : r + 1, here]
+                    * (prefix[r, :, here] + jnp.exp(-rate * seg_start) * carry[r : r + 1, here])
+                )
+
+            def step(j, states):
+                at = pl.ds(pl.multiple_of(j * SEGS, SEGS), SEGS)
+                states = [state * decay for state, decay in zip(states, decays)]
+                gates[at, here] = gates[at, here] * (y_local[at, here] + tree(list(states)))
+                return states
+
+            lax.fori_loop(0, steps, step, states, unroll=4)
+
+        here = pl.ds(q * part, part)
+        blocks[0, q] = jnp.dot(
+            turn_back[...], gates[:, here].astype(jnp.bfloat16), preferred_element_type=jnp.float32
+        ).astype(jnp.bfloat16)
+        a_x[q].start()
+        a_z[q].start()
+
+    weights[0] = w_ref[...]
+    pass_weight(0)
+    pass_weight(1)
+    pass_block(0)
+    pass_block(1)
+    pass_weight(2)
+    pass_block(2)
+    pass_block(3)
+    pass_weight(3)
+    for q in range(PARTS):
+        w_y[q].wait_recv()
+    for q in range(PARTS):
+        w_on[q].wait_recv()
+
+    def to_sibling(i, k):
+        return send(to_core.at[i, k], from_core.at[i, k], c_sems, i * 4 + k, {"ch": 1 - core})
+
+    def columns(k):
+        mask = (k % 2) * ZHI + (k // 2) * Y
+        return pl.ds(pl.multiple_of((me ^ mask) * cols, cols), cols)
+
+    def to_owner(i, k):
+        return send(
+            final.at[i, k], out_ref.at[:, columns(k)], o_sems, i * 4 + k, {"seq": me ^ ROW_MASKS[i]}
+        )
+
+    def finish(i):
+        @pl.loop(0, 4)
+        def _(k):
+            to_sibling(i, k).wait_recv()
+            total = acc[i % 2, k, pl.ds(pl.multiple_of(core * half, half), half), :] + from_core[
+                i, k
+            ].astype(jnp.float32)
+            if i == 0:
+                out_ref[:, columns(k)] = total.astype(jnp.bfloat16)
+            else:
+                final[i, k] = total.astype(jnp.bfloat16)
+                to_owner(i, k).start()
+
+    for i in range(4):
+        for q in range(PARTS):
+            if i == 1 and q % 2 == 1:
+                a_x[q].wait_recv()
+            if i == 2 and q % 2 == 0:
+                a_z[q].wait_recv()
+            if i == 3:
+                a_on[q].wait_recv()
+
+        @pl.loop(0, 4)
+        def _(k):
+            total = None
+            for q in range(PARTS):
+                term = jnp.dot(
+                    blocks[i, q],
+                    weights[k, pl.ds(q * part, part), :],
+                    preferred_element_type=jnp.float32,
+                )
+                total = term if total is None else total + term
+            acc[i % 2, k] = total
+            other = pl.ds(pl.multiple_of((1 - core) * half, half), half)
+            to_core[i, k] = acc[i % 2, k, other, :].astype(jnp.bfloat16)
+            to_sibling(i, k).start()
+
+        if i > 0:
+            finish(i - 1)
+    finish(3)
+
+    for i in range(1, 4):
+
+        @pl.loop(0, 4)
+        def _(k):
+            to_owner(i, k).wait_recv()
+            to_owner(i, k).wait_send()
+
+    for i in range(4):
+
+        @pl.loop(0, 4)
+        def _(k):
+            to_sibling(i, k).wait_send()
+
+    for group in (w_zhi, w_y, w_on, a_x, a_z, a_on):
+        for copy in group:
+            copy.wait_send()
+
+
+def fused(gate_input, key_input, value_input, rates, amps, out_weight):
+    rows, chans = gate_input.shape
+    poles = rates.shape[0]
+    cols = out_weight.shape[1]
+    half, part = rows // 2, chans // PARTS
+    vmem = pl.BlockSpec(memory_space=pltpu.VMEM)
+    f32, bf16 = jnp.float32, jnp.bfloat16
+    dma = pltpu.SemaphoreType.DMA
+    return pl.pallas_call(
+        fused_kernel,
+        out_shape=jax.ShapeDtypeStruct((half, 16 * cols), bf16),
+        in_specs=[vmem] * 6,
+        out_specs=vmem,
+        scratch_shapes=[
+            pltpu.VMEM((rows, rows), bf16),
+            pltpu.VMEM((rows, rows), bf16),
+            pltpu.VMEM((rows, chans), f32),
+            pltpu.VMEM((rows, chans), f32),
+            pltpu.VMEM((rows, chans), f32),
+            pltpu.VMEM((poles, SEGS, chans), f32),
+            pltpu.VMEM((poles, chans), f32),
+            pltpu.VMEM((4, poles, chans), f32),
+            pltpu.VMEM((4, poles, chans), f32),
+            pltpu.VMEM((4, chans, cols), bf16),
+            pltpu.VMEM((4, PARTS, rows, part), bf16),
+            pltpu.VMEM((2, 4, rows, cols), f32),
+            pltpu.VMEM((4, 4, half, cols), bf16),
+            pltpu.VMEM((4, 4, half, cols), bf16),
+            pltpu.VMEM((4, 4, half, cols), bf16),
+            dma((3 * PARTS,)),
+            dma((3 * PARTS,)),
+            dma((3 * PARTS,)),
+            dma((3 * PARTS,)),
+            dma((4,)),
+            dma((4,)),
+            dma((16,)),
+            dma((16,)),
+            dma((16,)),
+            dma((16,)),
+        ],
+        compiler_params=pltpu.CompilerParams(
+            collective_id=0, has_side_effects=True, vmem_limit_bytes=48 * 1024 * 1024
+        ),
+        cost_estimate=pl.CostEstimate(
+            flops=2 * 4 * rows * 4 * cols * chans, bytes_accessed=8 * rows * chans, transcendentals=0
+        ),
+        name="fused",
+    )(key_input, value_input, gate_input, rates, amps, out_weight)
 
 
 def body(gate_input, key_input, value_input, decay_rate, residues, out_weight):
-    shards = lax.axis_size("seq")
     rates = decay_rate.T
     amps = residues.T * jnp.sqrt(rates)
-    rows = gate_input.shape[0]
-    cols = out_weight.shape[1]
-    if shards != 16:
-        weight = lax.all_gather(out_weight, "seq", axis=1, tiled=True)
-        gated = conv_and_gate(gate_input, key_input, value_input, rates, amps)
-        return lax.psum_scatter(
-            jnp.dot(gated, weight, preferred_element_type=jnp.float32).astype(jnp.bfloat16),
-            "ch",
-            scatter_dimension=0,
-            tiled=True,
-        )
-    by_row, by_col = groups_of(shards, 5), groups_of(shards, 10)
-    weight = lax.all_gather(out_weight, "seq", axis=1, tiled=True, axis_index_groups=by_col)
+    if lax.axis_size("seq") == 16 and lax.axis_size("ch") == 2:
+        return fused(gate_input, key_input, value_input, rates, amps, out_weight)
+    weight = lax.all_gather(out_weight, "seq", axis=1, tiled=True)
     gated = conv_and_gate(gate_input, key_input, value_input, rates, amps)
-    gated = lax.all_gather(gated, "seq", axis=0, tiled=True, axis_index_groups=by_row)
-    part = jnp.dot(gated, weight, preferred_element_type=jnp.float32).astype(jnp.bfloat16)
-    part = part.reshape(4, rows, 4 * cols)
-    part = lax.psum_scatter(part, "ch", scatter_dimension=1, tiled=True)
-    part = lax.all_to_all(
-        part, "seq", split_axis=0, concat_axis=0, tiled=True, axis_index_groups=by_row
+    return lax.psum_scatter(
+        jnp.dot(gated, weight, preferred_element_type=jnp.float32).astype(jnp.bfloat16),
+        "ch",
+        scatter_dimension=0,
+        tiled=True,
     )
-    own = part.shape[1]
-    part = part.reshape(2, 2, own, 2, 2, cols)
-    return part.transpose(2, 3, 0, 4, 1, 5).reshape(own, shards * cols)
 
 
 def solution(mesh):

time: 302 us -> 122 us (0.40)
  waiting for transfers between devices: 234 us -> 0 us
  Pallas kernels: 15.4 us -> 115 us
  blocking collectives: 18.5 us -> 0 us
  between operations: 13.2 us -> 0.03 us
  matrix products: 9.32 us -> 0 us
    all_gather x3 -> x0, waiting for transfers between devices: 221 us -> none  [the longest x1 79.8 us: body(): lax.all_gather(gated, 'seq', axis=0, tiled=True, axis_index_groups=by_row)]
    pallas_call x2 -> x1, Pallas kernels: 15.4 us -> 115 us  [fused(): pl.pallas_call(fused_kernel, out_shape=jax.ShapeDtypeStruct((half, 16 * c...]
    all_to_all x1 -> x0, blocking collectives: 18.5 us -> none  [body(): lax.all_to_all(part, 'seq', split_axis=0, concat_axis=0, tiled=True, axis...]
    reduce_scatter x1 -> x0, waiting for transfers between devices: 11.5 us -> none  [body(): part = lax.psum_scatter(part, 'ch', scatter_dimension=1, tiled=True)]
    dot_general x1 -> x0, matrix products: 9.32 us -> none  [body(): jnp.dot(gated, weight, preferred_element_type=jnp.float32)]
    reshape x3 -> x0, local copies, waits for them, and re-layouts: 4.01 us -> none  [the longest x2 2.4 us: body(): part = part.reshape(2, 2, own, 2, 2, cols)]
  transfers between devices with their start and end apart: 4 -> 0, of which waited for: 4 -> 0; matrix products, arithmetic and copies ran while one was open for 1% -> 0% of each run, Pallas kernels for 2% -> 0%
where the time goes in v2:
time: 122 us
  Pallas kernels  115 us (94%)
  local copies, waits for them, and re-layouts  5.87 us (5%)
    pallas_call x1, Pallas kernels, fused(): pl.pallas_call(fused_kernel, out_shape=jax.ShapeDtypeStruct((half, 16 * c...  115 us
    unnamed x11, local copies, waits for them, and re-layouts  5.87 us

profile of v2, /device:TPU:0, one launch (start us, length us, event | category | flops | bytes accessed | tf_op | source)
XLA Modules:
  0.0 121.6 jit_solution(13732484462604772435)
XLA Ops:
  0.0 0.0 copy-start
  0.0 1.0 bitcast_multiply_fusion.amp_ref
  1.0 0.0 copy-done
  1.1 0.0 copy-start.1
  1.1 1.2 copy-done.1
  2.3 0.0 copy-start.2
  2.3 1.2 %copy-done.2 = bf16[256,2048]{1,0:T(8,128)(2,1)S(1)} copy-done((bf16[256,2048]{1,0:T(8,128)(2,1)S(1)}, bf16[256,2048]{1,0:T(8,128)(2,1)}, u32[]{:S(2)}) %copy-start.2) | copy-done | bytes 1048600
  3.5 0.0 copy-start.3
  3.5 1.2 %copy-done.3 = bf16[256,2048]{1,0:T(8,128)(2,1)S(1)} copy-done((bf16[256,2048]{1,0:T(8,128)(2,1)S(1)}, bf16[256,2048]{1,0:T(8,128)(2,1)}, u32[]{:S(2)}) %copy-start.3) | copy-done | bytes 1048600
  4.7 0.0 copy-start.4
  4.7 1.2 %copy-done.4 = bf16[2048,256]{1,0:T(8,128)(2,1)S(1)} copy-done((bf16[2048,256]{1,0:T(8,128)(2,1)S(1)}, bf16[2048,256]{1,0:T(8,128)(2,1)}, u32[]{:S(2)}) %copy-start.4) | copy-done | bytes 1048600
  6.0 114.7 %fused.1 = bf16[128,4096]{1,0:T(8,128)(2,1)S(1)} custom-call(bf16[256,2048]{1,0:T(8,128)(2,1)S(1)} %copy-done.1, bf16[256,2048]{1,0:T(8,128)(2,1)S(1)} %copy-done.2, bf16[256,2048]{1,0:T(8,128)(2,1)S(1)} %copy-done.3, f32[16,2048]{1,0:T(8,128)S(1)} %bitcast.4, f32[16,2048]{1,0:T(8,128)S(1)} %bitcast_multiply_fusion.amp_ref, bf16[2048,256]{1,0:T(8,128)(2,1)S(1)} %copy-done.4), custom_call_target="tpu_custom_call" | custom-call | flops 4294967296 | bytes 4194304 | tf_op jit(solution)/shard_map/fused/pallas_call | solution.py:414
  120.7 1.0 copy.8
Async XLA Ops:
  0.0 1.1 copy-start
  1.1 1.2 %copy-start.1 = (bf16[256,2048]{1,0:T(8,128)(2,1)S(1)}, bf16[256,2048]{1,0:T(8,128)(2,1)}, u32[]{:S(2)}) copy-start(bf16[256,2048]{1,0:T(8,128)(2,1)} %k_ref.1) | copy-start | bytes 3145732
  2.3 1.2 %copy-start.2 = (bf16[256,2048]{1,0:T(8,128)(2,1)S(1)}, bf16[256,2048]{1,0:T(8,128)(2,1)}, u32[]{:S(2)}) copy-start(bf16[256,2048]{1,0:T(8,128)(2,1)} %v_ref.1) | copy-start | bytes 3145732
  3.5 1.2 %copy-start.3 = (bf16[256,2048]{1,0:T(8,128)(2,1)S(1)}, bf16[256,2048]{1,0:T(8,128)(2,1)}, u32[]{:S(2)}) copy-start(bf16[256,2048]{1,0:T(8,128)(2,1)} %gate_ref.1) | copy-start | bytes 3145732
  4.7 1.2 %copy-start.4 = (bf16[2048,256]{1,0:T(8,128)(2,1)S(1)}, bf16[2048,256]{1,0:T(8,128)(2,1)}, u32[]{:S(2)}) copy-start(bf16[2048,256]{1,0:T(8,128)(2,1)} %w_ref.1) | copy-start | bytes 3145732

commit v3 on v2

--- a/solution.py
+++ b/solution.py
@@ -139,7 +139,6 @@
 MESH = pl.DeviceIdType.MESH
 X, Y, ZLO, ZHI = 1, 2, 4, 8
 ROW_MASKS = (0, X, ZLO, X | ZLO)
-COL_MASKS = (0, ZHI, Y, Y | ZHI)
 PARTS = 4
 
 
@@ -185,9 +184,8 @@
         w_zhi.append(send(mine, piece(1, q), w_sems, q, {"seq": me ^ ZHI}))
         w_y.append(send(mine, piece(2, q), w_sems, PARTS + q, {"seq": me ^ Y}))
         w_on.append(send(piece(1, q), piece(3, q), w_sems, 2 * PARTS + q, {"seq": me ^ Y}))
-    for q in range(PARTS):
-        w_zhi[q].start()
-        w_y[q].start()
+    w_zhi[0].start()
+    w_y[0].start()
 
     turn[...] = shuffle_matrix(rows, False)
     turn_back[...] = shuffle_matrix(rows, True)
@@ -254,6 +252,12 @@
     for bit in range(4):
         swap = send(held.at[bit], got.at[bit], s_sems, bit, {"seq": me ^ (1 << bit)})
         swap.start()
+        if bit == 1:
+            for q in range(1, PARTS):
+                w_y[q].start()
+        if bit == 3:
+            for q in range(1, PARTS):
+                w_zhi[q].start()
         local_part(bit)
         swap.wait()
         theirs = got[bit]
@@ -318,20 +322,6 @@
         a_x[q].start()
         a_z[q].start()
 
-    weights[0] = w_ref[...]
-    pass_weight(0)
-    pass_weight(1)
-    pass_block(0)
-    pass_block(1)
-    pass_weight(2)
-    pass_block(2)
-    pass_block(3)
-    pass_weight(3)
-    for q in range(PARTS):
-        w_y[q].wait_recv()
-    for q in range(PARTS):
-        w_on[q].wait_recv()
-
     def to_sibling(i, k):
         return send(to_core.at[i, k], from_core.at[i, k], c_sems, i * 4 + k, {"ch": 1 - core})
 
@@ -344,30 +334,10 @@
             final.at[i, k], out_ref.at[:, columns(k)], o_sems, i * 4 + k, {"seq": me ^ ROW_MASKS[i]}
         )
 
-    def finish(i):
-        @pl.loop(0, 4)
-        def _(k):
-            to_sibling(i, k).wait_recv()
-            total = acc[i % 2, k, pl.ds(pl.multiple_of(core * half, half), half), :] + from_core[
-                i, k
-            ].astype(jnp.float32)
-            if i == 0:
-                out_ref[:, columns(k)] = total.astype(jnp.bfloat16)
-            else:
-                final[i, k] = total.astype(jnp.bfloat16)
-                to_owner(i, k).start()
-
-    for i in range(4):
-        for q in range(PARTS):
-            if i == 1 and q % 2 == 1:
-                a_x[q].wait_recv()
-            if i == 2 and q % 2 == 0:
-                a_z[q].wait_recv()
-            if i == 3:
-                a_on[q].wait_recv()
-
-        @pl.loop(0, 4)
-        def _(k):
+    def multiply(i, first, count, stride=1):
+        @pl.loop(0, count)
+        def _(at):
+            k = first + at * stride
             total = None
             for q in range(PARTS):
                 term = jnp.dot(
@@ -376,14 +346,64 @@
                     preferred_element_type=jnp.float32,
                 )
                 total = term if total is None else total + term
-            acc[i % 2, k] = total
+            acc[i, k] = total
             other = pl.ds(pl.multiple_of((1 - core) * half, half), half)
-            to_core[i, k] = acc[i % 2, k, other, :].astype(jnp.bfloat16)
+            to_core[i, k] = acc[i, k, other, :].astype(jnp.bfloat16)
             to_sibling(i, k).start()
 
-        if i > 0:
-            finish(i - 1)
-    finish(3)
+    def finish(i, first, count, stride=1):
+        @pl.loop(0, count)
+        def _(at):
+            k = first + at * stride
+            to_sibling(i, k).wait_recv()
+            own = pl.ds(pl.multiple_of(core * half, half), half)
+            total = acc[i, k, own, :] + from_core[i, k].astype(jnp.float32)
+            if i == 0:
+                out_ref[:, columns(k)] = total.astype(jnp.bfloat16)
+            else:
+                final[i, k] = total.astype(jnp.bfloat16)
+                to_owner(i, k).start()
+
+    weights[0] = w_ref[...]
+    pass_weight(0)
+    multiply(0, 0, 1)
+    pass_weight(1)
+    pass_block(0)
+    pass_block(1)
+    finish(0, 0, 1)
+    for q in range(PARTS):
+        w_y[q].wait_recv()
+    multiply(0, 2, 1)
+    pass_weight(2)
+    pass_block(2)
+    pass_block(3)
+    finish(0, 2, 1)
+    for q in range(PARTS):
+        (a_z if q % 2 == 0 else a_x)[q].wait_recv()
+    multiply(1, 0, 2, 2)
+    pass_weight(3)
+    multiply(2, 0, 2, 2)
+    finish(1, 0, 2, 2)
+    multiply(0, 1, 1)
+    finish(2, 0, 2, 2)
+    multiply(1, 1, 1)
+    multiply(2, 1, 1)
+    finish(0, 1, 1)
+    finish(1, 1, 1)
+    for q in range(PARTS):
+        w_on[q].wait_recv()
+    multiply(1, 3, 1)
+    finish(2, 1, 1)
+    multiply(2, 3, 1)
+    finish(1, 3, 1)
+    multiply(0, 3, 1)
+    finish(2, 3, 1)
+    for q in range(PARTS):
+        a_on[q].wait_recv()
+    multiply(3, 0, 2)
+    finish(0, 3, 1)
+    multiply(3, 2, 2)
+    finish(3, 0, 4)
 
     for i in range(1, 4):
 
@@ -428,7 +448,7 @@
             pltpu.VMEM((4, poles, chans), f32),
             pltpu.VMEM((4, chans, cols), bf16),
             pltpu.VMEM((4, PARTS, rows, part), bf16),
-            pltpu.VMEM((2, 4, rows, cols), f32),
+            pltpu.VMEM((4, 4, rows, cols), f32),
             pltpu.VMEM((4, 4, half, cols), bf16),
             pltpu.VMEM((4, 4, half, cols), bf16),
             pltpu.VMEM((4, 4, half, cols), bf16),

time: 122 us -> 101 us (0.83)
  Pallas kernels: 115 us -> 93.5 us
    pallas_call x1, Pallas kernels: 115 us -> 93.5 us  [fused(): pl.pallas_call(fused_kernel, out_shape=jax.ShapeDtypeStruct((half, 16 * c...]
where the time goes in v3:
time: 101 us; the launch traced here: 100 us
  Pallas kernels  93.5 us (93%)
  local copies, waits for them, and re-layouts  5.87 us (6%)
  other arithmetic  1.04 us (1%)
    pallas_call x1, Pallas kernels, fused(): pl.pallas_call(fused_kernel, out_shape=jax.ShapeDtypeStruct((half, 16 * c...  93.5 us
    unnamed x11, local copies, waits for them, and re-layouts  5.87 us

profile of v3, /device:TPU:0, one launch (start us, length us, event | category | flops | bytes accessed | tf_op | source)
XLA Modules:
  0.0 100.4 jit_solution(153207590732027315)
XLA Ops:
  0.0 0.0 copy-start
  0.0 1.0 %bitcast_multiply_fusion.amp_ref = f32[16,2048]{1,0:T(8,128)S(1)} fusion(f32[2048,16]{0,1:T(8,128)} %param.10, f32[2048,16]{0,1:T(8,128)} %param.9), kind=kLoop, calls=%fused_computation | loop fusion | flops 32768 | bytes 393216 | tf_op jit(solution)/shard_map/mul | solution.py:478
  1.0 0.0 copy-done
  1.1 0.0 copy-start.1
  1.1 1.2 %copy-done.1 = bf16[256,2048]{1,0:T(8,128)(2,1)S(1)} copy-done((bf16[256,2048]{1,0:T(8,128)(2,1)S(1)}, bf16[256,2048]{1,0:T(8,128)(2,1)}, u32[]{:S(2)}) %copy-start.1) | copy-done | bytes 1048600
  2.3 0.0 copy-start.2
  2.3 1.2 %copy-done.2 = bf16[256,2048]{1,0:T(8,128)(2,1)S(1)} copy-done((bf16[256,2048]{1,0:T(8,128)(2,1)S(1)}, bf16[256,2048]{1,0:T(8,128)(2,1)}, u32[]{:S(2)}) %copy-start.2) | copy-done | bytes 1048600
  3.5 0.0 copy-start.3
  3.5 1.2 %copy-done.3 = bf16[256,2048]{1,0:T(8,128)(2,1)S(1)} copy-done((bf16[256,2048]{1,0:T(8,128)(2,1)S(1)}, bf16[256,2048]{1,0:T(8,128)(2,1)}, u32[]{:S(2)}) %copy-start.3) | copy-done | bytes 1048600
  4.7 0.0 copy-start.4
  4.7 1.2 %copy-done.4 = bf16[2048,256]{1,0:T(8,128)(2,1)S(1)} copy-done((bf16[2048,256]{1,0:T(8,128)(2,1)S(1)}, bf16[2048,256]{1,0:T(8,128)(2,1)}, u32[]{:S(2)}) %copy-start.4) | copy-done | bytes 1048600
  6.0 93.5 %fused.1 = bf16[128,4096]{1,0:T(8,128)(2,1)S(1)} custom-call(bf16[256,2048]{1,0:T(8,128)(2,1)S(1)} %copy-done.1, bf16[256,2048]{1,0:T(8,128)(2,1)S(1)} %copy-done.2, bf16[256,2048]{1,0:T(8,128)(2,1)S(1)} %copy-done.3, f32[16,2048]{1,0:T(8,128)S(1)} %bitcast.4, f32[16,2048]{1,0:T(8,128)S(1)} %bitcast_multiply_fusion.amp_ref, bf16[2048,256]{1,0:T(8,128)(2,1)S(1)} %copy-done.4), custom_call_target="tpu_custom_call" | custom-call | flops 4294967296 | bytes 4194304 | tf_op jit(solution)/shard_map/fused/pallas_call | solution.py:434
  99.4 1.0 copy.8
Async XLA Ops:
  0.0 1.1 %copy-start = (f32[2048,16]{0,1:T(8,128)S(1)}, f32[2048,16]{0,1:T(8,128)}, u32[]{:S(2)}) copy-start(f32[2048,16]{0,1:T(8,128)} %param.9) | copy-start | bytes 393220
  1.1 1.2 %copy-start.1 = (bf16[256,2048]{1,0:T(8,128)(2,1)S(1)}, bf16[256,2048]{1,0:T(8,128)(2,1)}, u32[]{:S(2)}) copy-start(bf16[256,2048]{1,0:T(8,128)(2,1)} %k_ref.1) | copy-start | bytes 3145732
  2.3 1.2 %copy-start.2 = (bf16[256,2048]{1,0:T(8,128)(2,1)S(1)}, bf16[256,2048]{1,0:T(8,128)(2,1)}, u32[]{:S(2)}) copy-start(bf16[256,2048]{1,0:T(8,128)(2,1)} %v_ref.1) | copy-start | bytes 3145732
  3.5 1.2 %copy-start.3 = (bf16[256,2048]{1,0:T(8,128)(2,1)S(1)}, bf16[256,2048]{1,0:T(8,128)(2,1)}, u32[]{:S(2)}) copy-start(bf16[256,2048]{1,0:T(8,128)(2,1)} %gate_ref.1) | copy-start | bytes 3145732
  4.7 1.2 %copy-start.4 = (bf16[2048,256]{1,0:T(8,128)(2,1)S(1)}, bf16[2048,256]{1,0:T(8,128)(2,1)}, u32[]{:S(2)}) copy-start(bf16[2048,256]{1,0:T(8,128)(2,1)} %w_ref.1) | copy-start | bytes 3145732

commit v4 on v3

--- a/solution.py
+++ b/solution.py
@@ -140,21 +140,39 @@
 X, Y, ZLO, ZHI = 1, 2, 4, 8
 ROW_MASKS = (0, X, ZLO, X | ZLO)
 PARTS = 4
+CHUNKS = 8
 
 
 def fused_kernel(
-    k_ref, v_ref, gate_ref, rate_ref, amp_ref, w_ref, out_ref,
-    turn, turn_back, signal, y_local, gates, prefix, carry, held, got,
+    k_hbm, v_hbm, gate_hbm, rate_ref, amp_ref, w_ref, out_ref,
+    k_ref, v_ref, gate_ref, turn, turn_back, signal, y_local, gates, prefix, carry, held, got,
     weights, blocks, acc, to_core, from_core, final,
-    w_send, w_recv, a_send, a_recv, s_send, s_recv, c_send, c_recv, o_send, o_recv,
+    load_sem, w_send, w_recv, a_send, a_recv, s_send, s_recv, c_send, c_recv, o_send, o_recv,
 ):
-    rows, chans = k_ref.shape
+    rows, chans = gates.shape
     poles = rate_ref.shape[0]
     cols = w_ref.shape[1]
     steps = rows // SEGS
     part = chans // PARTS
+    chunk = chans // CHUNKS
     half = rows // 2
     me, core = lax.axis_index("seq"), lax.axis_index("ch")
+
+    loads = []
+    for q in range(PARTS):
+        here = pl.ds(q * part, part)
+        loads.append(
+            [
+                pltpu.make_async_copy(src.at[:, here], dst.at[q], load_sem.at[n * PARTS + q])
+                for n, (src, dst) in enumerate(
+                    ((k_hbm, k_ref), (v_hbm, v_ref), (gate_hbm, gate_ref))
+                )
+            ]
+        )
+        for load in loads[q]:
+            load.start()
+    own_weight = pltpu.make_async_copy(w_ref, weights.at[0], load_sem.at[3 * PARTS])
+    own_weight.start()
 
     barrier = pltpu.get_barrier_semaphore()
     for mask in (X, Y, ZLO, ZHI, X | ZLO):
@@ -175,31 +193,30 @@
     w_sems, a_sems, s_sems = (w_send, w_recv), (a_send, a_recv), (s_send, s_recv)
     c_sems, o_sems = (c_send, c_recv), (o_send, o_recv)
 
-    def piece(slot, q):
-        return weights.at[slot, pl.ds(q * part, part), :]
+    def piece(slot, n):
+        return weights.at[slot, pl.ds(n * chunk, chunk), :]
 
     w_zhi, w_y, w_on = [], [], []
-    for q in range(PARTS):
-        mine = w_ref.at[pl.ds(q * part, part), :]
-        w_zhi.append(send(mine, piece(1, q), w_sems, q, {"seq": me ^ ZHI}))
-        w_y.append(send(mine, piece(2, q), w_sems, PARTS + q, {"seq": me ^ Y}))
-        w_on.append(send(piece(1, q), piece(3, q), w_sems, 2 * PARTS + q, {"seq": me ^ Y}))
-    w_zhi[0].start()
-    w_y[0].start()
+    for n in range(CHUNKS):
+        mine = w_ref.at[pl.ds(n * chunk, chunk), :]
+        w_zhi.append(send(mine, piece(1, n), w_sems, n, {"seq": me ^ ZHI}))
+        w_y.append(send(mine, piece(2, n), w_sems, CHUNKS + n, {"seq": me ^ Y}))
+        w_on.append(send(piece(1, n), piece(3, n), w_sems, 2 * CHUNKS + n, {"seq": me ^ Y}))
+
+    def start_some(copies, first, last):
+        for copy in copies[first:last]:
+            copy.start()
+
+    start_some(w_zhi, 0, 2)
+    start_some(w_y, 0, 2)
 
     turn[...] = shuffle_matrix(rows, False)
     turn_back[...] = shuffle_matrix(rows, True)
-
-    @pl.loop(0, PARTS)
-    def _(q):
-        here = pl.ds(pl.multiple_of(q * part, part), part)
-        signal[:, here] = jnp.dot(
-            turn[...], k_ref[:, here], preferred_element_type=jnp.float32
-        ) * jnp.dot(turn[...], v_ref[:, here], preferred_element_type=jnp.float32)
 
     seg = lax.broadcasted_iota(jnp.int32, (SEGS, LANES), 0)
     seg_start = seg.astype(jnp.float32) * float(steps)
     zeros = [jnp.zeros((SEGS, LANES), jnp.float32)] * poles
+    lanes = part // LANES
 
     def tree(terms):
         while len(terms) > 1:
@@ -209,30 +226,40 @@
     def wide(ref, r, here):
         return jnp.broadcast_to(ref[r : r + 1, here], (SEGS, LANES))
 
-    @pl.loop(0, chans // LANES)
-    def _(lane):
-        here = pl.ds(pl.multiple_of(lane * LANES, LANES), LANES)
-        decays = [jnp.exp(-wide(rate_ref, r, here)) for r in range(poles)]
-
-        def step(j, states):
-            at = pl.ds(pl.multiple_of(j * SEGS, SEGS), SEGS)
-            new = signal[at, here]
-            return [state * decay + new for state, decay in zip(states, decays)]
-
-        states = lax.fori_loop(0, steps, step, zeros, unroll=4)
-        for r in range(poles):
-            run = states[r]
-            rate = wide(rate_ref, r, here)
-            for hop in (1, 2, 4):
-                back = jnp.where(seg >= hop, pltpu.roll(run, hop, 0), 0.0)
-                run = run + back * jnp.exp(rate * float(-steps * hop))
-            held[0, r : r + 1, here] = run[SEGS - 1 : SEGS, :]
-            prefix[r, :, here] = jnp.where(seg >= 1, pltpu.roll(run, 1, 0), 0.0)
+    def lane_at(lane):
+        return pl.ds(pl.multiple_of(lane * LANES, LANES), LANES)
+
+    def state_pass(q):
+        loads[q][0].wait()
+        loads[q][1].wait()
+        signal[:, pl.ds(q * part, part)] = jnp.dot(
+            turn[...], k_ref[q], preferred_element_type=jnp.float32
+        ) * jnp.dot(turn[...], v_ref[q], preferred_element_type=jnp.float32)
+
+        @pl.loop(0, lanes)
+        def _(lane):
+            here, inner = lane_at(q * lanes + lane), lane_at(lane)
+            decays = [jnp.exp(-wide(rate_ref, r, here)) for r in range(poles)]
+
+            def step(j, states):
+                at = pl.ds(pl.multiple_of(j * SEGS, SEGS), SEGS)
+                new = signal[at, here]
+                return [state * decay + new for state, decay in zip(states, decays)]
+
+            states = lax.fori_loop(0, steps, step, zeros, unroll=4)
+            for r in range(poles):
+                run = states[r]
+                rate = wide(rate_ref, r, here)
+                for hop in (1, 2, 4):
+                    back = jnp.where(seg >= hop, pltpu.roll(run, hop, 0), 0.0)
+                    run = run + back * jnp.exp(rate * float(-steps * hop))
+                held[q, 0, r : r + 1, inner] = run[SEGS - 1 : SEGS, :]
+                prefix[r, :, here] = jnp.where(seg >= 1, pltpu.roll(run, 1, 0), 0.0)
 
     def local_part(q):
-        @pl.loop(q * (part // LANES), (q + 1) * (part // LANES))
+        @pl.loop(0, lanes)
         def _(lane):
-            here = pl.ds(pl.multiple_of(lane * LANES, LANES), LANES)
+            here = lane_at(q * lanes + lane)
             decays = [jnp.exp(-wide(rate_ref, r, here)) for r in range(poles)]
             amps = [wide(amp_ref, r, here) for r in range(poles)]
 
@@ -245,31 +272,28 @@
 
             lax.fori_loop(0, steps, step, zeros, unroll=4)
 
+        loads[q][2].wait()
+        gates[:, pl.ds(q * part, part)] = jnp.dot(
+            turn[...], gate_ref[q], preferred_element_type=jnp.float32
+        )
+
+    def swap(q, bit):
+        return send(
+            held.at[q, bit], got.at[q, bit], s_sems, q * 4 + bit, {"seq": me ^ (1 << bit)}
+        )
+
+    def absorb(q, bit):
+        theirs = got[q, bit]
         here = pl.ds(q * part, part)
-        gates[:, here] = jnp.dot(turn[...], gate_ref[:, here], preferred_element_type=jnp.float32)
-
-    carry[...] = jnp.zeros_like(carry)
-    for bit in range(4):
-        swap = send(held.at[bit], got.at[bit], s_sems, bit, {"seq": me ^ (1 << bit)})
-        swap.start()
-        if bit == 1:
-            for q in range(1, PARTS):
-                w_y[q].start()
-        if bit == 3:
-            for q in range(1, PARTS):
-                w_zhi[q].start()
-        local_part(bit)
-        swap.wait()
-        theirs = got[bit]
-        rate = rate_ref[...]
-        later = (me // (1 << bit)) % 2
-        later_f = later.astype(jnp.float32)
+        rate = rate_ref[:, here]
+        later = ((me // (1 << bit)) % 2).astype(jnp.float32)
         before = (me % (1 << bit)).astype(jnp.float32) * float(rows)
         span = float(rows << bit)
-        carry[...] = carry[...] + later_f * (jnp.exp(-rate * before) * theirs)
+        more = later * (jnp.exp(-rate * before) * theirs)
+        carry[:, here] = more if bit == 0 else carry[:, here] + more
         if bit < 3:
-            held[bit + 1] = held[bit] * jnp.exp(-rate * (span * (1.0 - later_f))) + theirs * jnp.exp(
-                -rate * (span * later_f)
+            held[q, bit + 1] = held[q, bit] * jnp.exp(-rate * (span * (1.0 - later))) + (
+                theirs * jnp.exp(-rate * (span * later))
             )
 
     a_x, a_z, a_on = [], [], []
@@ -285,19 +309,18 @@
                 send(blocks.at[2, q], blocks.at[3, q], a_sems, 2 * PARTS + q, {"seq": me ^ X})
             )
 
-    def pass_weight(q):
-        w_zhi[q].wait_recv()
-        w_on[q].start()
+    def pass_weight(n):
+        w_zhi[n].wait_recv()
+        w_on[n].start()
 
     def pass_block(q):
         (a_x if q % 2 == 0 else a_z)[q].wait_recv()
         a_on[q].start()
 
-    for q in range(PARTS):
-
-        @pl.loop(q * (part // LANES), (q + 1) * (part // LANES))
+    def gate_part(q):
+        @pl.loop(0, lanes)
         def _(lane):
-            here = pl.ds(pl.multiple_of(lane * LANES, LANES), LANES)
+            here = lane_at(q * lanes + lane)
             decays, states = [], []
             for r in range(poles):
                 rate = wide(rate_ref, r, here)
@@ -321,6 +344,29 @@
         ).astype(jnp.bfloat16)
         a_x[q].start()
         a_z[q].start()
+
+    state_pass(0)
+    for wave in range(PARTS + 4):
+        moving = [(q, wave - q) for q in range(PARTS) if 0 <= wave - q < 4]
+        for q, bit in moving:
+            swap(q, bit).start()
+        if wave == 3:
+            start_some(w_zhi, 2, 3)
+        if wave == 4:
+            start_some(w_y, 2, CHUNKS)
+        if wave == 6:
+            start_some(w_zhi, 3, CHUNKS)
+        if wave + 1 < PARTS:
+            state_pass(wave + 1)
+        if 0 <= wave - 1 < PARTS:
+            local_part(wave - 1)
+        if 0 <= wave - 4 < PARTS:
+            gate_part(wave - 4)
+        if wave in (5, 7):
+            pass_weight((wave - 5) // 2)
+        for q, bit in moving:
+            swap(q, bit).wait()
+            absorb(q, bit)
 
     def to_sibling(i, k):
         return send(to_core.at[i, k], from_core.at[i, k], c_sems, i * 4 + k, {"ch": 1 - core})
@@ -364,34 +410,36 @@
                 final[i, k] = total.astype(jnp.bfloat16)
                 to_owner(i, k).start()
 
-    weights[0] = w_ref[...]
-    pass_weight(0)
+    own_weight.wait()
     multiply(0, 0, 1)
-    pass_weight(1)
     pass_block(0)
+    pass_weight(2)
     pass_block(1)
     finish(0, 0, 1)
-    for q in range(PARTS):
-        w_y[q].wait_recv()
+    pass_weight(3)
+    pass_block(2)
+    for n in range(CHUNKS):
+        w_y[n].wait_recv()
     multiply(0, 2, 1)
-    pass_weight(2)
-    pass_block(2)
+    pass_weight(4)
     pass_block(3)
     finish(0, 2, 1)
+    pass_weight(5)
     for q in range(PARTS):
         (a_z if q % 2 == 0 else a_x)[q].wait_recv()
     multiply(1, 0, 2, 2)
-    pass_weight(3)
+    pass_weight(6)
     multiply(2, 0, 2, 2)
     finish(1, 0, 2, 2)
+    pass_weight(7)
     multiply(0, 1, 1)
     finish(2, 0, 2, 2)
     multiply(1, 1, 1)
     multiply(2, 1, 1)
     finish(0, 1, 1)
     finish(1, 1, 1)
-    for q in range(PARTS):
-        w_on[q].wait_recv()
+    for n in range(CHUNKS):
+        w_on[n].wait_recv()
     multiply(1, 3, 1)
     finish(2, 1, 1)
     multiply(2, 3, 1)
@@ -429,14 +477,18 @@
     cols = out_weight.shape[1]
     half, part = rows // 2, chans // PARTS
     vmem = pl.BlockSpec(memory_space=pltpu.VMEM)
+    hbm = pl.BlockSpec(memory_space=pl.ANY)
     f32, bf16 = jnp.float32, jnp.bfloat16
     dma = pltpu.SemaphoreType.DMA
     return pl.pallas_call(
         fused_kernel,
         out_shape=jax.ShapeDtypeStruct((half, 16 * cols), bf16),
-        in_specs=[vmem] * 6,
+        in_specs=[hbm] * 3 + [vmem] * 2 + [hbm],
         out_specs=vmem,
         scratch_shapes=[
+            pltpu.VMEM((PARTS, rows, part), bf16),
+            pltpu.VMEM((PARTS, rows, part), bf16),
+            pltpu.VMEM((PARTS, rows, part), bf16),
             pltpu.VMEM((rows, rows), bf16),
             pltpu.VMEM((rows, rows), bf16),
             pltpu.VMEM((rows, chans), f32),
@@ -444,27 +496,28 @@
             pltpu.VMEM((rows, chans), f32),
             pltpu.VMEM((poles, SEGS, chans), f32),
             pltpu.VMEM((poles, chans), f32),
-            pltpu.VMEM((4, poles, chans), f32),
-            pltpu.VMEM((4, poles, chans), f32),
+            pltpu.VMEM((PARTS, 4, poles, part), f32),
+            pltpu.VMEM((PARTS, 4, poles, part), f32),
             pltpu.VMEM((4, chans, cols), bf16),
             pltpu.VMEM((4, PARTS, rows, part), bf16),
             pltpu.VMEM((4, 4, rows, cols), f32),
             pltpu.VMEM((4, 4, half, cols), bf16),
             pltpu.VMEM((4, 4, half, cols), bf16),
             pltpu.VMEM((4, 4, half, cols), bf16),
+            dma((3 * PARTS + 1,)),
+            dma((3 * CHUNKS,)),
+            dma((3 * CHUNKS,)),
             dma((3 * PARTS,)),
             dma((3 * PARTS,)),
-            dma((3 * PARTS,)),
-            dma((3 * PARTS,)),
-            dma((4,)),
-            dma((4,)),
+            dma((4 * PARTS,)),
+            dma((4 * PARTS,)),
             dma((16,)),
             dma((16,)),
             dma((16,)),
             dma((16,)),
         ],
         compiler_params=pltpu.CompilerParams(
-            collective_id=0, has_side_effects=True, vmem_limit_bytes=48 * 1024 * 1024
+            collective_id=0, has_side_effects=True, vmem_limit_bytes=60 * 1024 * 1024
         ),
         cost_estimate=pl.CostEstimate(
             flops=2 * 4 * rows * 4 * cols * chans, bytes_accessed=8 * rows * chans, transcendentals=0

time: 101 us -> 97.4 us (0.964)
  local copies, waits for them, and re-layouts: 5.87 us -> 2.29 us
    unnamed x11 -> x1, local copies, waits for them, and re-layouts: 5.87 us -> 2.29 us
where the time goes in v4:
time: 97.4 us; the launch traced here: 97.2 us
  Pallas kernels  93.3 us (96%)
  local copies, waits for them, and re-layouts  2.29 us (2%)
  other arithmetic  1.66 us (2%)
    pallas_call x1, Pallas kernels, fused(): pl.pallas_call(fused_kernel, out_shape=jax.ShapeDtypeStruct((half, 16 * c...  93.3 us
    unnamed x1, local copies, waits for them, and re-layouts  2.29 us

profile of v4, /device:TPU:0, one launch (start us, length us, event | category | flops | bytes accessed | tf_op | source)
XLA Modules:
  0.0 97.2 jit_solution(11472783747650456992)
XLA Ops:
  0.0 1.7 %bitcast_multiply_fusion.amp_ref = f32[16,2048]{1,0:T(8,128)} fusion(f32[2048,16]{0,1:T(8,128)} %param.10, f32[2048,16]{0,1:T(8,128)} %param.9), kind=kLoop, calls=%fused_computation | loop fusion | flops 32768 | bytes 393216 | tf_op jit(solution)/shard_map/mul | solution.py:531
  1.7 93.3 %fused.1 = bf16[128,4096]{1,0:T(8,128)(2,1)} custom-call(bf16[256,2048]{1,0:T(8,128)(2,1)} %k_hbm.1, bf16[256,2048]{1,0:T(8,128)(2,1)} %v_hbm.1, bf16[256,2048]{1,0:T(8,128)(2,1)} %gate_hbm.1, f32[16,2048]{1,0:T(8,128)} %bitcast.4, f32[16,2048]{1,0:T(8,128)} %bitcast_multiply_fusion.amp_ref, bf16[2048,256]{1,0:T(8,128)(2,1)} %w_ref.1), custom_call_target="tpu_custom_call" | custom-call | flops 4294967296 | bytes 4194304 | tf_op jit(solution)/shard_map/fused/pallas_call | solution.py:483
  94.9 2.3 %copy.8 = bf16[128,4096]{1,0:T(8,128)(2,1)} copy(bf16[128,4096]{1,0:T(8,128)(2,1)} %fused.1) | data formatting | bytes 2097152

commit v5 on v4

--- a/solution.py
+++ b/solution.py
@@ -141,6 +141,7 @@
 ROW_MASKS = (0, X, ZLO, X | ZLO)
 PARTS = 4
 CHUNKS = 8
+X_FIRST = (3,)
 
 
 def fused_kernel(
@@ -207,7 +208,7 @@
         for copy in copies[first:last]:
             copy.start()
 
-    start_some(w_zhi, 0, 2)
+    start_some(w_zhi, 0, 3)
     start_some(w_y, 0, 2)
 
     turn[...] = shuffle_matrix(rows, False)
@@ -300,7 +301,7 @@
     for q in range(PARTS):
         a_x.append(send(blocks.at[0, q], blocks.at[1, q], a_sems, q, {"seq": me ^ X}))
         a_z.append(send(blocks.at[0, q], blocks.at[2, q], a_sems, PARTS + q, {"seq": me ^ ZLO}))
-        if q % 2 == 0:
+        if q in X_FIRST:
             a_on.append(
                 send(blocks.at[1, q], blocks.at[3, q], a_sems, 2 * PARTS + q, {"seq": me ^ ZLO})
             )
@@ -314,7 +315,7 @@
         w_on[n].start()
 
     def pass_block(q):
-        (a_x if q % 2 == 0 else a_z)[q].wait_recv()
+        (a_x if q in X_FIRST else a_z)[q].wait_recv()
         a_on[q].start()
 
     def gate_part(q):
@@ -350,12 +351,11 @@
         moving = [(q, wave - q) for q in range(PARTS) if 0 <= wave - q < 4]
         for q, bit in moving:
             swap(q, bit).start()
-        if wave == 3:
-            start_some(w_zhi, 2, 3)
         if wave == 4:
             start_some(w_y, 2, CHUNKS)
+            start_some(w_zhi, 3, 4)
         if wave == 6:
-            start_some(w_zhi, 3, CHUNKS)
+            start_some(w_zhi, 4, CHUNKS)
         if wave + 1 < PARTS:
             state_pass(wave + 1)
         if 0 <= wave - 1 < PARTS:
@@ -412,46 +412,48 @@
 
     own_weight.wait()
     multiply(0, 0, 1)
+    pass_weight(2)
     pass_block(0)
-    pass_weight(2)
+    pass_weight(3)
+    finish(0, 0, 1)
+    pass_weight(4)
+    pass_weight(5)
     pass_block(1)
-    finish(0, 0, 1)
-    pass_weight(3)
-    pass_block(2)
+    pass_block(3)
+    for q in range(PARTS):
+        if q not in X_FIRST:
+            a_x[q].wait_recv()
+    pass_weight(6)
+    multiply(1, 0, 1)
     for n in range(CHUNKS):
         w_y[n].wait_recv()
-    multiply(0, 2, 1)
-    pass_weight(4)
-    pass_block(3)
-    finish(0, 2, 1)
-    pass_weight(5)
-    for q in range(PARTS):
-        (a_z if q % 2 == 0 else a_x)[q].wait_recv()
-    multiply(1, 0, 2, 2)
-    pass_weight(6)
-    multiply(2, 0, 2, 2)
+    multiply(1, 2, 1)
     finish(1, 0, 2, 2)
     pass_weight(7)
-    multiply(0, 1, 1)
-    finish(2, 0, 2, 2)
     multiply(1, 1, 1)
-    multiply(2, 1, 1)
-    finish(0, 1, 1)
+    multiply(0, 1, 2)
     finish(1, 1, 1)
+    pass_block(2)
+    finish(0, 1, 2)
+    for q in X_FIRST:
+        a_z[q].wait_recv()
+    multiply(2, 0, 3)
     for n in range(CHUNKS):
         w_on[n].wait_recv()
+    multiply(2, 3, 1)
+    finish(2, 0, 4)
     multiply(1, 3, 1)
-    finish(2, 1, 1)
-    multiply(2, 3, 1)
+    multiply(0, 3, 1)
     finish(1, 3, 1)
-    multiply(0, 3, 1)
-    finish(2, 3, 1)
     for q in range(PARTS):
         a_on[q].wait_recv()
     multiply(3, 0, 2)
     finish(0, 3, 1)
-    multiply(3, 2, 2)
-    finish(3, 0, 4)
+    finish(3, 0, 1)
+    multiply(3, 2, 1)
+    finish(3, 1, 1)
+    multiply(3, 3, 1)
+    finish(3, 2, 2)
 
     for i in range(1, 4):
 
@@ -517,7 +519,7 @@
             dma((16,)),
         ],
         compiler_params=pltpu.CompilerParams(
-            collective_id=0, has_side_effects=True, vmem_limit_bytes=60 * 1024 * 1024
+            collective_id=0, has_side_effects=True, vmem_limit_bytes=40 * 1024 * 1024
         ),
         cost_estimate=pl.CostEstimate(
             flops=2 * 4 * rows * 4 * cols * chans, bytes_accessed=8 * rows * chans, transcendentals=0

time: 97.4 us -> 93.3 us (0.958)
  Pallas kernels: 93.3 us -> 86.1 us
  local copies, waits for them, and re-layouts: 2.29 us -> 5.87 us
    pallas_call x1, Pallas kernels: 93.3 us -> 86.1 us  [fused(): pl.pallas_call(fused_kernel, out_shape=jax.ShapeDtypeStruct((half, 16 * c...]
    unnamed x1 -> x11, local copies, waits for them, and re-layouts: 2.29 us -> 5.87 us
where the time goes in v5:
time: 93.3 us; the launch traced here: 93 us
  Pallas kernels  86.1 us (92%)
  local copies, waits for them, and re-layouts  5.87 us (6%)
  other arithmetic  1.04 us (1%)
    pallas_call x1, Pallas kernels, fused(): pl.pallas_call(fused_kernel, out_shape=jax.ShapeDtypeStruct((half, 16 * c...  86.1 us
    unnamed x11, local copies, waits for them, and re-layouts  5.87 us

profile of v5, /device:TPU:0, one launch (start us, length us, event | category | flops | bytes accessed | tf_op | source)
XLA Modules:
  0.0 93.0 jit_solution(384835671018300856)
XLA Ops:
  0.0 0.0 copy-start
  0.0 1.0 %bitcast_multiply_fusion.amp_ref = f32[16,2048]{1,0:T(8,128)S(1)} fusion(f32[2048,16]{0,1:T(8,128)} %param.10, f32[2048,16]{0,1:T(8,128)} %param.9), kind=kLoop, calls=%fused_computation | loop fusion | flops 32768 | bytes 393216 | tf_op jit(solution)/shard_map/mul | solution.py:533
  1.0 0.0 copy-done
  1.1 0.0 copy-start.1
  1.1 1.2 %copy-done.1 = bf16[256,2048]{1,0:T(8,128)(2,1)S(1)} copy-done((bf16[256,2048]{1,0:T(8,128)(2,1)S(1)}, bf16[256,2048]{1,0:T(8,128)(2,1)}, u32[]{:S(2)}) %copy-start.1) | copy-done | bytes 1048600
  2.3 0.0 copy-start.2
  2.3 1.2 %copy-done.2 = bf16[256,2048]{1,0:T(8,128)(2,1)S(1)} copy-done((bf16[256,2048]{1,0:T(8,128)(2,1)S(1)}, bf16[256,2048]{1,0:T(8,128)(2,1)}, u32[]{:S(2)}) %copy-start.2) | copy-done | bytes 1048600
  3.5 0.0 copy-start.3
  3.5 1.2 %copy-done.3 = bf16[256,2048]{1,0:T(8,128)(2,1)S(1)} copy-done((bf16[256,2048]{1,0:T(8,128)(2,1)S(1)}, bf16[256,2048]{1,0:T(8,128)(2,1)}, u32[]{:S(2)}) %copy-start.3) | copy-done | bytes 1048600
  4.7 0.0 copy-start.4
  4.7 1.2 %copy-done.4 = bf16[2048,256]{1,0:T(8,128)(2,1)S(1)} copy-done((bf16[2048,256]{1,0:T(8,128)(2,1)S(1)}, bf16[2048,256]{1,0:T(8,128)(2,1)}, u32[]{:S(2)}) %copy-start.4) | copy-done | bytes 1048600
  6.0 86.1 %fused.1 = bf16[128,4096]{1,0:T(8,128)(2,1)S(1)} custom-call(bf16[256,2048]{1,0:T(8,128)(2,1)S(1)} %copy-done.1, bf16[256,2048]{1,0:T(8,128)(2,1)S(1)} %copy-done.2, bf16[256,2048]{1,0:T(8,128)(2,1)S(1)} %copy-done.3, f32[16,2048]{1,0:T(8,128)S(1)} %bitcast.4, f32[16,2048]{1,0:T(8,128)S(1)} %bitcast_multiply_fusion.amp_ref, bf16[2048,256]{1,0:T(8,128)(2,1)S(1)} %copy-done.4), custom_call_target="tpu_custom_call" | custom-call | flops 4294967296 | bytes 4194304 | tf_op jit(solution)/shard_map/fused/pallas_call | solution.py:485
  92.1 1.0 %copy.8 = bf16[128,4096]{1,0:T(8,128)(2,1)} copy(bf16[128,4096]{1,0:T(8,128)(2,1)S(1)} %fused.1) | data formatting | bytes 2097152
Async XLA Ops:
  0.0 1.1 %copy-start = (f32[2048,16]{0,1:T(8,128)S(1)}, f32[2048,16]{0,1:T(8,128)}, u32[]{:S(2)}) copy-start(f32[2048,16]{0,1:T(8,128)} %param.9) | copy-start | bytes 393220
  1.1 1.2 %copy-start.1 = (bf16[256,2048]{1,0:T(8,128)(2,1)S(1)}, bf16[256,2048]{1,0:T(8,128)(2,1)}, u32[]{:S(2)}) copy-start(bf16[256,2048]{1,0:T(8,128)(2,1)} %k_hbm.1) | copy-start | bytes 3145732
  2.3 1.2 %copy-start.2 = (bf16[256,2048]{1,0:T(8,128)(2,1)S(1)}, bf16[256,2048]{1,0:T(8,128)(2,1)}, u32[]{:S(2)}) copy-start(bf16[256,2048]{1,0:T(8,128)(2,1)} %v_hbm.1) | copy-start | bytes 3145732
  3.5 1.2 %copy-start.3 = (bf16[256,2048]{1,0:T(8,128)(2,1)S(1)}, bf16[256,2048]{1,0:T(8,128)(2,1)}, u32[]{:S(2)}) copy-start(bf16[256,2048]{1,0:T(8,128)(2,1)} %gate_hbm.1) | copy-start | bytes 3145732
  4.7 1.2 %copy-start.4 = (bf16[2048,256]{1,0:T(8,128)(2,1)S(1)}, bf16[2048,256]{1,0:T(8,128)(2,1)}, u32[]{:S(2)}) copy-start(bf16[2048,256]{1,0:T(8,128)(2,1)} %w_ref.1) | copy-start | bytes 3145732

commit v6 on v4

--- a/solution.py
+++ b/solution.py
@@ -138,7 +138,9 @@
 
 MESH = pl.DeviceIdType.MESH
 X, Y, ZLO, ZHI = 1, 2, 4, 8
-ROW_MASKS = (0, X, ZLO, X | ZLO)
+ROW_MASKS = (0, X, Y, X | Y)
+PLANES = 4
+AREA = 4
 PARTS = 4
 CHUNKS = 8
 
@@ -147,7 +149,7 @@
     k_hbm, v_hbm, gate_hbm, rate_ref, amp_ref, w_ref, out_ref,
     k_ref, v_ref, gate_ref, turn, turn_back, signal, y_local, gates, prefix, carry, held, got,
     weights, blocks, acc, to_core, from_core, final,
-    load_sem, w_send, w_recv, a_send, a_recv, s_send, s_recv, c_send, c_recv, o_send, o_recv,
+    load_sem, up_send, up_recv, down_send, down_recv, a_send, a_recv, s_send, s_recv, c_send, c_recv, o_send, o_recv,
 ):
     rows, chans = gates.shape
     poles = rate_ref.shape[0]
@@ -157,6 +159,7 @@
     chunk = chans // CHUNKS
     half = rows // 2
     me, core = lax.axis_index("seq"), lax.axis_index("ch")
+    plane = me // AREA
 
     loads = []
     for q in range(PARTS):
@@ -171,14 +174,16 @@
         )
         for load in loads[q]:
             load.start()
-    own_weight = pltpu.make_async_copy(w_ref, weights.at[0], load_sem.at[3 * PARTS])
+    own_weight = pltpu.make_async_copy(w_ref, weights.at[plane], load_sem.at[3 * PARTS])
     own_weight.start()
 
     barrier = pltpu.get_barrier_semaphore()
-    for mask in (X, Y, ZLO, ZHI, X | ZLO):
-        pl.semaphore_signal(barrier, inc=1, device_id={"seq": me ^ mask}, device_id_type=MESH)
+    for place in (
+        me ^ X, me ^ Y, me ^ (X | Y), me ^ ZHI, (me + AREA) % (PLANES * AREA), (me + 3 * AREA) % (PLANES * AREA)
+    ):
+        pl.semaphore_signal(barrier, inc=1, device_id={"seq": place}, device_id_type=MESH)
     pl.semaphore_signal(barrier, inc=1, device_id={"ch": 1 - core}, device_id_type=MESH)
-    pl.semaphore_wait(barrier, 6)
+    pl.semaphore_wait(barrier, 7)
 
     def send(src, dst, sems, place, target):
         return pltpu.make_async_remote_copy(
@@ -190,25 +195,54 @@
             device_id_type=MESH,
         )
 
-    w_sems, a_sems, s_sems = (w_send, w_recv), (a_send, a_recv), (s_send, s_recv)
+    a_sems, s_sems = (a_send, a_recv), (s_send, s_recv)
     c_sems, o_sems = (c_send, c_recv), (o_send, o_recv)
 
-    def piece(slot, n):
-        return weights.at[slot, pl.ds(n * chunk, chunk), :]
-
-    w_zhi, w_y, w_on = [], [], []
-    for n in range(CHUNKS):
-        mine = w_ref.at[pl.ds(n * chunk, chunk), :]
-        w_zhi.append(send(mine, piece(1, n), w_sems, n, {"seq": me ^ ZHI}))
-        w_y.append(send(mine, piece(2, n), w_sems, CHUNKS + n, {"seq": me ^ Y}))
-        w_on.append(send(piece(1, n), piece(3, n), w_sems, 2 * CHUNKS + n, {"seq": me ^ Y}))
-
-    def start_some(copies, first, last):
-        for copy in copies[first:last]:
-            copy.start()
-
-    start_some(w_zhi, 0, 2)
-    start_some(w_y, 0, 2)
+    def hop(up, far, n):
+        at = pl.ds(n * chunk, chunk)
+        slot = plane - far if up else plane + far
+        src = w_ref.at[at, :] if far == 0 else weights.at[slot, at, :]
+        sems = (up_send, up_recv) if up else (down_send, down_recv)
+        target = {"seq": me + AREA if up else me - AREA}
+        return send(src, weights.at[slot, at, :], sems, far * CHUNKS + n, target)
+
+    def has_next(up):
+        return plane < PLANES - 1 if up else plane > 0
+
+    def has_block(up, far):
+        return plane >= far if up else plane < PLANES - far
+
+    def start_own(n):
+        for up in (True, False):
+
+            @pl.when(has_next(up))
+            def _():
+                hop(up, 0, n).start()
+
+    def arrived(far, n):
+        for up in (True, False):
+
+            @pl.when(has_block(up, far))
+            def _():
+                at = pl.ds(n * chunk, chunk)
+                slot = plane - far if up else plane + far
+                sems = (up_send, up_recv) if up else (down_send, down_recv)
+                send(
+                    weights.at[slot, at, :],
+                    weights.at[slot, at, :],
+                    sems,
+                    (far - 1) * CHUNKS + n,
+                    {"seq": me ^ ZHI},
+                ).wait_recv()
+
+            if far < PLANES - 1:
+
+                @pl.when(jnp.logical_and(has_block(up, far), has_next(up)))
+                def _():
+                    hop(up, far, n).start()
+
+    for n in range(3):
+        start_own(n)
 
     turn[...] = shuffle_matrix(rows, False)
     turn_back[...] = shuffle_matrix(rows, True)
@@ -296,25 +330,21 @@
                 theirs * jnp.exp(-rate * (span * later))
             )
 
-    a_x, a_z, a_on = [], [], []
+    a_x, a_y, a_on = [], [], []
     for q in range(PARTS):
         a_x.append(send(blocks.at[0, q], blocks.at[1, q], a_sems, q, {"seq": me ^ X}))
-        a_z.append(send(blocks.at[0, q], blocks.at[2, q], a_sems, PARTS + q, {"seq": me ^ ZLO}))
+        a_y.append(send(blocks.at[0, q], blocks.at[2, q], a_sems, PARTS + q, {"seq": me ^ Y}))
         if q % 2 == 0:
             a_on.append(
-                send(blocks.at[1, q], blocks.at[3, q], a_sems, 2 * PARTS + q, {"seq": me ^ ZLO})
+                send(blocks.at[1, q], blocks.at[3, q], a_sems, 2 * PARTS + q, {"seq": me ^ Y})
             )
         else:
             a_on.append(
                 send(blocks.at[2, q], blocks.at[3, q], a_sems, 2 * PARTS + q, {"seq": me ^ X})
             )
 
-    def pass_weight(n):
-        w_zhi[n].wait_recv()
-        w_on[n].start()
-
     def pass_block(q):
-        (a_x if q % 2 == 0 else a_z)[q].wait_recv()
+        (a_x if q % 2 == 0 else a_y)[q].wait_recv()
         a_on[q].start()
 
     def gate_part(q):
@@ -343,27 +373,23 @@
             turn_back[...], gates[:, here].astype(jnp.bfloat16), preferred_element_type=jnp.float32
         ).astype(jnp.bfloat16)
         a_x[q].start()
-        a_z[q].start()
+        a_y[q].start()
 
     state_pass(0)
     for wave in range(PARTS + 4):
         moving = [(q, wave - q) for q in range(PARTS) if 0 <= wave - q < 4]
         for q, bit in moving:
             swap(q, bit).start()
-        if wave == 3:
-            start_some(w_zhi, 2, 3)
-        if wave == 4:
-            start_some(w_y, 2, CHUNKS)
-        if wave == 6:
-            start_some(w_zhi, 3, CHUNKS)
+        if wave < CHUNKS - 3:
+            start_own(wave + 3)
         if wave + 1 < PARTS:
             state_pass(wave + 1)
         if 0 <= wave - 1 < PARTS:
             local_part(wave - 1)
         if 0 <= wave - 4 < PARTS:
             gate_part(wave - 4)
-        if wave in (5, 7):
-            pass_weight((wave - 5) // 2)
+        if wave >= 4:
+            arrived(1, wave - 4)
         for q, bit in moving:
             swap(q, bit).wait()
             absorb(q, bit)
@@ -372,86 +398,102 @@
         return send(to_core.at[i, k], from_core.at[i, k], c_sems, i * 4 + k, {"ch": 1 - core})
 
     def columns(k):
-        mask = (k % 2) * ZHI + (k // 2) * Y
-        return pl.ds(pl.multiple_of((me ^ mask) * cols, cols), cols)
+        return pl.ds(pl.multiple_of((k * AREA + me % AREA) * cols, cols), cols)
 
     def to_owner(i, k):
         return send(
             final.at[i, k], out_ref.at[:, columns(k)], o_sems, i * 4 + k, {"seq": me ^ ROW_MASKS[i]}
         )
 
-    def multiply(i, first, count, stride=1):
-        @pl.loop(0, count)
-        def _(at):
-            k = first + at * stride
-            total = None
-            for q in range(PARTS):
-                term = jnp.dot(
-                    blocks[i, q],
-                    weights[k, pl.ds(q * part, part), :],
-                    preferred_element_type=jnp.float32,
-                )
-                total = term if total is None else total + term
-            acc[i, k] = total
-            other = pl.ds(pl.multiple_of((1 - core) * half, half), half)
-            to_core[i, k] = acc[i, k, other, :].astype(jnp.bfloat16)
-            to_sibling(i, k).start()
-
-    def finish(i, first, count, stride=1):
-        @pl.loop(0, count)
-        def _(at):
-            k = first + at * stride
-            to_sibling(i, k).wait_recv()
-            own = pl.ds(pl.multiple_of(core * half, half), half)
-            total = acc[i, k, own, :] + from_core[i, k].astype(jnp.float32)
-            if i == 0:
-                out_ref[:, columns(k)] = total.astype(jnp.bfloat16)
-            else:
-                final[i, k] = total.astype(jnp.bfloat16)
-                to_owner(i, k).start()
+    def multiply(i, k):
+        total = None
+        for q in range(PARTS):
+            term = jnp.dot(
+                blocks[i, q],
+                weights[k, pl.ds(q * part, part), :],
+                preferred_element_type=jnp.float32,
+            )
+            total = term if total is None else total + term
+        acc[i, k] = total
+        other = pl.ds(pl.multiple_of((1 - core) * half, half), half)
+        to_core[i, k] = acc[i, k, other, :].astype(jnp.bfloat16)
+        to_sibling(i, k).start()
+
+    def finish(i, k):
+        to_sibling(i, k).wait_recv()
+        own = pl.ds(pl.multiple_of(core * half, half), half)
+        total = acc[i, k, own, :] + from_core[i, k].astype(jnp.float32)
+        if i == 0:
+            out_ref[:, columns(k)] = total.astype(jnp.bfloat16)
+        else:
+            final[i, k] = total.astype(jnp.bfloat16)
+            to_owner(i, k).start()
+
+    def tiles(work, i, far):
+        if far == 0:
+            work(i, plane)
+            return
+
+        @pl.loop(0, 2)
+        def _(side):
+            k = plane + (2 * side - 1) * far
+
+            @pl.when(jnp.logical_and(k >= 0, k < PLANES))
+            def _():
+                work(i, k)
 
     own_weight.wait()
-    multiply(0, 0, 1)
+    tiles(multiply, 0, 0)
+    arrived(1, 4)
     pass_block(0)
-    pass_weight(2)
+    arrived(1, 5)
     pass_block(1)
-    finish(0, 0, 1)
-    pass_weight(3)
+    arrived(1, 6)
+    tiles(finish, 0, 0)
+    arrived(1, 7)
+    arrived(2, 0)
     pass_block(2)
-    for n in range(CHUNKS):
-        w_y[n].wait_recv()
-    multiply(0, 2, 1)
-    pass_weight(4)
+    arrived(2, 1)
+    arrived(2, 2)
     pass_block(3)
-    finish(0, 2, 1)
-    pass_weight(5)
+    arrived(2, 3)
+    tiles(multiply, 0, 1)
     for q in range(PARTS):
-        (a_z if q % 2 == 0 else a_x)[q].wait_recv()
-    multiply(1, 0, 2, 2)
-    pass_weight(6)
-    multiply(2, 0, 2, 2)
-    finish(1, 0, 2, 2)
-    pass_weight(7)
-    multiply(0, 1, 1)
-    finish(2, 0, 2, 2)
-    multiply(1, 1, 1)
-    multiply(2, 1, 1)
-    finish(0, 1, 1)
-    finish(1, 1, 1)
-    for n in range(CHUNKS):
-        w_on[n].wait_recv()
-    multiply(1, 3, 1)
-    finish(2, 1, 1)
-    multiply(2, 3, 1)
-    finish(1, 3, 1)
-    multiply(0, 3, 1)
-    finish(2, 3, 1)
+        (a_y if q % 2 == 0 else a_x)[q].wait_recv()
+    arrived(2, 4)
+    tiles(multiply, 1, 0)
+    tiles(finish, 0, 1)
+    tiles(multiply, 1, 1)
+    arrived(2, 5)
+    tiles(multiply, 2, 0)
+    tiles(finish, 1, 0)
+    tiles(finish, 1, 1)
+    arrived(2, 6)
+    tiles(multiply, 2, 1)
+    tiles(finish, 2, 0)
+    arrived(2, 7)
+    tiles(multiply, 1, 2)
+    tiles(finish, 2, 1)
+    tiles(multiply, 2, 2)
+    tiles(finish, 1, 2)
+    tiles(multiply, 0, 2)
+    tiles(finish, 2, 2)
     for q in range(PARTS):
         a_on[q].wait_recv()
-    multiply(3, 0, 2)
-    finish(0, 3, 1)
-    multiply(3, 2, 2)
-    finish(3, 0, 4)
+    for far in range(3):
+        tiles(multiply, 3, far)
+        if far > 0:
+            tiles(finish, 3, far - 1)
+    tiles(finish, 0, 2)
+    tiles(finish, 3, 2)
+    for n in range(CHUNKS):
+        arrived(3, n)
+    for i in (3, 1, 2, 0):
+        tiles(multiply, i, 3)
+        if i in (1, 2):
+            tiles(finish, 3 if i == 1 else 1, 3)
+    tiles(finish, 2, 3)
+    tiles(finish, 0, 3)
 
     for i in range(1, 4):
 
@@ -466,9 +508,16 @@
         def _(k):
             to_sibling(i, k).wait_send()
 
-    for group in (w_zhi, w_y, w_on, a_x, a_z, a_on):
+    for group in (a_x, a_y, a_on):
         for copy in group:
             copy.wait_send()
+    for up in (True, False):
+        for far in range(PLANES - 1):
+
+            @pl.when(jnp.logical_and(has_block(up, far), has_next(up)))
+            def _():
+                for n in range(CHUNKS):
+                    hop(up, far, n).wait_send()
 
 
 def fused(gate_input, key_input, value_input, rates, amps, out_weight):
@@ -477,7 +526,7 @@
     cols = out_weight.shape[1]
     half, part = rows // 2, chans // PARTS
     vmem = pl.BlockSpec(memory_space=pltpu.VMEM)
-    hbm = pl.BlockSpec(memory_space=pl.ANY)
+    hbm = pl.BlockSpec(memory_space=pltpu.HBM)
     f32, bf16 = jnp.float32, jnp.bfloat16
     dma = pltpu.SemaphoreType.DMA
     return pl.pallas_call(
@@ -507,6 +556,8 @@
             dma((3 * PARTS + 1,)),
             dma((3 * CHUNKS,)),
             dma((3 * CHUNKS,)),
+            dma((3 * CHUNKS,)),
+            dma((3 * CHUNKS,)),
             dma((3 * PARTS,)),
             dma((3 * PARTS,)),
             dma((4 * PARTS,)),
@@ -517,7 +568,7 @@
             dma((16,)),
         ],
         compiler_params=pltpu.CompilerParams(
-            collective_id=0, has_side_effects=True, vmem_limit_bytes=60 * 1024 * 1024
+            collective_id=0, has_side_effects=True, vmem_limit_bytes=54 * 1024 * 1024
         ),
         cost_estimate=pl.CostEstimate(
             flops=2 * 4 * rows * 4 * cols * chans, bytes_accessed=8 * rows * chans, transcendentals=0

time: 97.4 us -> 95.4 us (0.979)
  Pallas kernels: 93.3 us -> 91.2 us
    pallas_call x1, Pallas kernels: 93.3 us -> 91.2 us  [fused(): pl.pallas_call(fused_kernel, out_shape=jax.ShapeDtypeStruct((half, 16 * c...]
where the time goes in v6:
time: 95.4 us; the launch traced here: 95.2 us
  Pallas kernels  91.2 us (96%)
  local copies, waits for them, and re-layouts  2.29 us (2%)
  other arithmetic  1.66 us (2%)
    pallas_call x1, Pallas kernels, fused(): pl.pallas_call(fused_kernel, out_shape=jax.ShapeDtypeStruct((half, 16 * c...  91.2 us
    unnamed x1, local copies, waits for them, and re-layouts  2.29 us

profile of v6, /device:TPU:0, one launch (start us, length us, event | category | flops | bytes accessed | tf_op | source)
XLA Modules:
  0.0 95.2 jit_solution(3400592124049604809)
XLA Ops:
  0.0 1.7 %bitcast_multiply_fusion.amp_ref = f32[16,2048]{1,0:T(8,128)} fusion(f32[2048,16]{0,1:T(8,128)} %param.10, f32[2048,16]{0,1:T(8,128)} %param.9), kind=kLoop, calls=%fused_computation | loop fusion | flops 32768 | bytes 393216 | tf_op jit(solution)/shard_map/mul | solution.py:582
  1.7 91.2 %fused.1 = bf16[128,4096]{1,0:T(8,128)(2,1)} custom-call(bf16[256,2048]{1,0:T(8,128)(2,1)} %k_hbm.1, bf16[256,2048]{1,0:T(8,128)(2,1)} %v_hbm.1, bf16[256,2048]{1,0:T(8,128)(2,1)} %gate_hbm.1, f32[16,2048]{1,0:T(8,128)} %bitcast.4, f32[16,2048]{1,0:T(8,128)} %bitcast_multiply_fusion.amp_ref, bf16[2048,256]{1,0:T(8,128)(2,1)} %w_ref.1), custom_call_target="tpu_custom_call" | custom-call | flops 4294967296 | bytes 4194304 | tf_op jit(solution)/shard_map/fused/pallas_call | solution.py:532
  92.9 2.3 %copy.8 = bf16[128,4096]{1,0:T(8,128)(2,1)} copy(bf16[128,4096]{1,0:T(8,128)(2,1)} %fused.1) | data formatting | bytes 2097152

commit v7 on v5

--- a/solution.py
+++ b/solution.py
@@ -380,6 +380,11 @@
             final.at[i, k], out_ref.at[:, columns(k)], o_sems, i * 4 + k, {"seq": me ^ ROW_MASKS[i]}
         )
 
+    def keep(k):
+        return pltpu.make_async_copy(
+            final.at[0, k], out_ref.at[:, columns(k)], load_sem.at[3 * PARTS + 1 + k]
+        )
+
     def multiply(i, first, count, stride=1):
         @pl.loop(0, count)
         def _(at):
@@ -404,10 +409,10 @@
             to_sibling(i, k).wait_recv()
             own = pl.ds(pl.multiple_of(core * half, half), half)
             total = acc[i, k, own, :] + from_core[i, k].astype(jnp.float32)
+            final[i, k] = total.astype(jnp.bfloat16)
             if i == 0:
-                out_ref[:, columns(k)] = total.astype(jnp.bfloat16)
+                keep(k).start()
             else:
-                final[i, k] = total.astype(jnp.bfloat16)
                 to_owner(i, k).start()
 
     own_weight.wait()
@@ -437,12 +442,15 @@
     finish(0, 1, 2)
     for q in X_FIRST:
         a_z[q].wait_recv()
-    multiply(2, 0, 3)
+    multiply(2, 0, 2)
+    finish(2, 0, 1)
+    multiply(2, 2, 1)
+    finish(2, 1, 2)
     for n in range(CHUNKS):
         w_on[n].wait_recv()
     multiply(2, 3, 1)
-    finish(2, 0, 4)
     multiply(1, 3, 1)
+    finish(2, 3, 1)
     multiply(0, 3, 1)
     finish(1, 3, 1)
     for q in range(PARTS):
@@ -461,6 +469,10 @@
         def _(k):
             to_owner(i, k).wait_recv()
             to_owner(i, k).wait_send()
+
+    @pl.loop(0, 4)
+    def _(k):
+        keep(k).wait()
 
     for i in range(4):
 
@@ -486,7 +498,7 @@
         fused_kernel,
         out_shape=jax.ShapeDtypeStruct((half, 16 * cols), bf16),
         in_specs=[hbm] * 3 + [vmem] * 2 + [hbm],
-        out_specs=vmem,
+        out_specs=hbm,
         scratch_shapes=[
             pltpu.VMEM((PARTS, rows, part), bf16),
             pltpu.VMEM((PARTS, rows, part), bf16),
@@ -506,7 +518,7 @@
             pltpu.VMEM((4, 4, half, cols), bf16),
             pltpu.VMEM((4, 4, half, cols), bf16),
             pltpu.VMEM((4, 4, half, cols), bf16),
-            dma((3 * PARTS + 1,)),
+            dma((3 * PARTS + 5,)),
             dma((3 * CHUNKS,)),
             dma((3 * CHUNKS,)),
             dma((3 * PARTS,)),
@@ -519,7 +531,7 @@
             dma((16,)),
         ],
         compiler_params=pltpu.CompilerParams(
-            collective_id=0, has_side_effects=True, vmem_limit_bytes=40 * 1024 * 1024
+            collective_id=0, has_side_effects=True, vmem_limit_bytes=54 * 1024 * 1024
         ),
         cost_estimate=pl.CostEstimate(
             flops=2 * 4 * rows * 4 * cols * chans, bytes_accessed=8 * rows * chans, transcendentals=0

time: 93.3 us -> 91.2 us (0.977)
  local copies, waits for them, and re-layouts: 5.87 us -> 2.29 us
  Pallas kernels: 86.1 us -> 87.1 us
    unnamed x11 -> x1, local copies, waits for them, and re-layouts: 5.87 us -> 2.29 us
    pallas_call x1, Pallas kernels: 86.1 us -> 87.1 us  [fused(): pl.pallas_call(fused_kernel, out_shape=jax.ShapeDtypeStruct((half, 16 * c...]
where the time goes in v7:
time: 91.2 us; the launch traced here: 91 us
  Pallas kernels  87.1 us (96%)
  local copies, waits for them, and re-layouts  2.29 us (3%)
  other arithmetic  1.66 us (2%)
    pallas_call x1, Pallas kernels, fused(): pl.pallas_call(fused_kernel, out_shape=jax.ShapeDtypeStruct((half, 16 * c...  87.1 us
    unnamed x1, local copies, waits for them, and re-layouts  2.29 us

profile of v7, /device:TPU:0, one launch (start us, length us, event | category | flops | bytes accessed | tf_op | source)
XLA Modules:
  0.0 91.0 jit_solution(3666234025298491884)
XLA Ops:
  0.0 1.7 %bitcast_multiply_fusion.amp_ref = f32[16,2048]{1,0:T(8,128)} fusion(f32[2048,16]{0,1:T(8,128)} %param.10, f32[2048,16]{0,1:T(8,128)} %param.9), kind=kLoop, calls=%fused_computation | loop fusion | flops 32768 | bytes 393216 | tf_op jit(solution)/shard_map/mul | solution.py:545
  1.7 87.1 %fused.1 = bf16[128,4096]{1,0:T(8,128)(2,1)} custom-call(bf16[256,2048]{1,0:T(8,128)(2,1)} %k_hbm.1, bf16[256,2048]{1,0:T(8,128)(2,1)} %v_hbm.1, bf16[256,2048]{1,0:T(8,128)(2,1)} %gate_hbm.1, f32[16,2048]{1,0:T(8,128)} %bitcast.4, f32[16,2048]{1,0:T(8,128)} %bitcast_multiply_fusion.amp_ref, bf16[2048,256]{1,0:T(8,128)(2,1)} %w_ref.1), custom_call_target="tpu_custom_call" | custom-call | flops 4294967296 | bytes 4194304 | tf_op jit(solution)/shard_map/fused/pallas_call | solution.py:497
  88.8 2.3 %copy.8 = bf16[128,4096]{1,0:T(8,128)(2,1)} copy(bf16[128,4096]{1,0:T(8,128)(2,1)} %fused.1) | data formatting | bytes 2097152

commit v8 on v7

--- a/solution.py
+++ b/solution.py
@@ -141,7 +141,6 @@
 ROW_MASKS = (0, X, ZLO, X | ZLO)
 PARTS = 4
 CHUNKS = 8
-X_FIRST = (3,)
 
 
 def fused_kernel(
@@ -301,21 +300,16 @@
     for q in range(PARTS):
         a_x.append(send(blocks.at[0, q], blocks.at[1, q], a_sems, q, {"seq": me ^ X}))
         a_z.append(send(blocks.at[0, q], blocks.at[2, q], a_sems, PARTS + q, {"seq": me ^ ZLO}))
-        if q in X_FIRST:
-            a_on.append(
-                send(blocks.at[1, q], blocks.at[3, q], a_sems, 2 * PARTS + q, {"seq": me ^ ZLO})
-            )
-        else:
-            a_on.append(
-                send(blocks.at[2, q], blocks.at[3, q], a_sems, 2 * PARTS + q, {"seq": me ^ X})
-            )
+        a_on.append(
+            send(blocks.at[2, q], blocks.at[3, q], a_sems, 2 * PARTS + q, {"seq": me ^ X})
+        )
 
     def pass_weight(n):
         w_zhi[n].wait_recv()
         w_on[n].start()
 
     def pass_block(q):
-        (a_x if q in X_FIRST else a_z)[q].wait_recv()
+        a_z[q].wait_recv()
         a_on[q].start()
 
     def gate_part(q):
@@ -424,10 +418,8 @@
     pass_weight(4)
     pass_weight(5)
     pass_block(1)
-    pass_block(3)
     for q in range(PARTS):
-        if q not in X_FIRST:
-            a_x[q].wait_recv()
+        a_x[q].wait_recv()
     pass_weight(6)
     multiply(1, 0, 1)
     for n in range(CHUNKS):
@@ -440,8 +432,7 @@
     finish(1, 1, 1)
     pass_block(2)
     finish(0, 1, 2)
-    for q in X_FIRST:
-        a_z[q].wait_recv()
+    pass_block(3)
     multiply(2, 0, 2)
     finish(2, 0, 1)
     multiply(2, 2, 1)

time: 91.2 us -> 96.8 us (1.061)
  Pallas kernels: 87.1 us -> 92.6 us
    pallas_call x1, Pallas kernels: 87.1 us -> 92.6 us  [fused(): pl.pallas_call(fused_kernel, out_shape=jax.ShapeDtypeStruct((half, 16 * c...]
where the time goes in v8:
time: 96.8 us; the launch traced here: 96.5 us
  Pallas kernels  92.6 us (96%)
  local copies, waits for them, and re-layouts  2.29 us (2%)
  other arithmetic  1.66 us (2%)
    pallas_call x1, Pallas kernels, fused(): pl.pallas_call(fused_kernel, out_shape=jax.ShapeDtypeStruct((half, 16 * c...  92.6 us
    unnamed x1, local copies, waits for them, and re-layouts  2.29 us

profile of v8, /device:TPU:0, one launch (start us, length us, event | category | flops | bytes accessed | tf_op | source)
XLA Modules:
  0.0 96.5 jit_solution(12069227587571206526)
XLA Ops:
  0.0 1.7 %bitcast_multiply_fusion.amp_ref = f32[16,2048]{1,0:T(8,128)} fusion(f32[2048,16]{0,1:T(8,128)} %param.10, f32[2048,16]{0,1:T(8,128)} %param.9), kind=kLoop, calls=%fused_computation | loop fusion | flops 32768 | bytes 393216 | tf_op jit(solution)/shard_map/mul | solution.py:536
  1.7 92.6 %fused.1 = bf16[128,4096]{1,0:T(8,128)(2,1)} custom-call(bf16[256,2048]{1,0:T(8,128)(2,1)} %k_hbm.1, bf16[256,2048]{1,0:T(8,128)(2,1)} %v_hbm.1, bf16[256,2048]{1,0:T(8,128)(2,1)} %gate_hbm.1, f32[16,2048]{1,0:T(8,128)} %bitcast.4, f32[16,2048]{1,0:T(8,128)} %bitcast_multiply_fusion.amp_ref, bf16[2048,256]{1,0:T(8,128)(2,1)} %w_ref.1), custom_call_target="tpu_custom_call" | custom-call | flops 4294967296 | bytes 4194304 | tf_op jit(solution)/shard_map/fused/pallas_call | solution.py:488
  94.2 2.3 %copy.8 = bf16[128,4096]{1,0:T(8,128)(2,1)} copy(bf16[128,4096]{1,0:T(8,128)(2,1)} %fused.1) | data formatting | bytes 2097152
